TPU v7x, 256 devices: a whole 4x4x8 slice. The times are simulated.
256 devices in a mesh: dp: 32 (over z_hi, y, x), owner: 8 (over z_lo, core).
Axes of the slice: x: 4, y: 4, z: 8 (z_hi: 2, z_lo: 4; z = z_hi * 4 + z_lo), core: 2. Of those that a mesh axis runs over, the one named last changes fastest.
Arguments:
- grad_partial: bfloat16 [32, 32, 1024, 1024], P('dp', None, 'owner')
- factor_stats: float32 [32, 8, 256, 1024], P('dp', 'owner'), as said below
- owner_table: int32 [32], P('dp'), may hold values from 0 to 7, as said below
Outputs:
- direction: float32 [32, 1024, 1024], P('dp', 'owner')
Inputs may be any that keep to these rules, and one draw needn't show every extreme that they name: `factor_stats`: left_stats and right_stats of every block are symmetric positive definite. `owner_table`: every slot is the first slot of the left factor of exactly 4 blocks.
All inputs are finite; a program needn't handle non-finite values.
Results may differ from a plain program's by a relative error of at most 0.0067.
Values may be sent and summed in bfloat16 or wider, within the bound.
No kernel may reach another device: no remote copies, remote signals or barrier semaphores. Data moves between devices by JAX's collectives and lax.ppermute only.
A program may use at most 128 MiB of HBM per device.

v0:
```python
import jax
import jax.numpy as jnp
from jax import lax
from jax.sharding import PartitionSpec as P


def spread(block, axis, owner):
    block = jnp.where(lax.axis_index(axis) == owner, block, jnp.zeros_like(block))
    return lax.psum(block, axis)


def start_terms(normed):
    rows, size = normed.shape
    row_ids = lax.broadcasted_iota(jnp.int32, (rows, size), 0)
    col_ids = lax.broadcasted_iota(jnp.int32, (rows, size), 1)
    eye_rows = jnp.where(row_ids == col_ids, 1.0, 0.0).astype(jnp.float32)
    start = normed.astype(jnp.bfloat16)
    first = (1.5 * eye_rows - 0.5 * normed).astype(jnp.bfloat16)
    return (start, first, eye_rows)


def whole_root(stats_mat):
    scale = jnp.sqrt(jnp.sum(stats_mat * stats_mat))
    start, first, eye_rows = start_terms(stats_mat / scale)
    second = jnp.dot(start, first, preferred_element_type=jnp.float32).astype(jnp.bfloat16)
    third = (
        1.5 * eye_rows - 0.5 * jnp.dot(first, second, preferred_element_type=jnp.float32)
    ).astype(jnp.bfloat16)
    return jnp.dot(third, first, preferred_element_type=jnp.float32).astype(jnp.bfloat16)


def spare_root(stats_mat):
    return jnp.zeros(stats_mat.shape, jnp.bfloat16)


def pick_slots(gathered, first_slot, count, owners):
    indices = (first_slot + jnp.arange(count, dtype=jnp.int32)) % owners
    chosen = jnp.take(gathered, indices, axis=0)
    return chosen.reshape(count * gathered.shape[1], gathered.shape[2])


def local(grad_partial, factor_stats, owner_table):
    owners = lax.axis_size("owner")
    halfway = owners // 2
    rows_here = grad_partial.shape[2]
    summed = lax.psum_scatter(
        grad_partial[0].astype(jnp.float32), "dp", scatter_dimension=0, tiled=True
    )
    grad_rows_bf = summed.astype(jnp.bfloat16)
    offset = owner_table[0]
    position = lax.axis_index("owner")
    step_pos = (position - offset) % owners
    is_right = step_pos >= halfway
    quarter = step_pos % halfway
    other_first = (offset + jnp.where(is_right, 0, halfway)) % owners
    right_first = (offset + halfway) % owners
    every_stats = lax.all_gather(factor_stats[0], "owner", axis=0, tiled=True)
    other_stats = pick_slots(every_stats, other_first, halfway, owners)
    other_root = lax.cond(quarter == 0, whole_root, spare_root, other_stats)
    left_root = spread(other_root, "owner", right_first)
    right_root = spread(other_root, "owner", offset)
    left_rows = lax.dynamic_slice_in_dim(left_root, position * rows_here, rows_here, 0)
    mixed = jnp.dot(
        left_rows,
        lax.all_gather(grad_rows_bf, "owner", axis=1, tiled=True)[0],
        preferred_element_type=jnp.float32,
    ).astype(jnp.bfloat16)
    precond = jnp.dot(mixed, right_root, preferred_element_type=jnp.float32)
    grad_wide = grad_rows_bf[0].astype(jnp.float32)
    grad_total, cond_total = lax.psum(
        (jnp.sum(grad_wide * grad_wide), jnp.sum(precond * precond)), "owner"
    )
    count = float(left_root.shape[0] * left_root.shape[1])
    factor = jnp.sqrt(grad_total / count / (cond_total / count + 1e-06))
    return (precond * factor)[None]


def solution(mesh):
    placed = (P("dp", None, "owner", None), P("dp", "owner", None, None), P("dp"))
    return jax.shard_map(
        local, mesh=mesh, in_specs=placed, out_specs=P("dp", "owner", None), check_vma=False
    )
```

profile of v0, /device:TPU:6, one launch (start us, length us, event | category | flops | bytes accessed | tf_op | source)
XLA Modules:
  0.0 626.6 jit_solution(8503329486240305213)
XLA Ops:
  7.4 0.0 all-gather.6.cloned.1.call-start
  7.4 0.7 all-gather.6.cloned.1.call-update
  8.1 0.0 reduce-scatter.2.cloned.1.call-start
  8.1 11.3 %bitcast_convert_fusion = f32[32,128,1024]{2,1,0:T(8,128)} fusion(bf16[1,32,128,1024]{3,2,1,0:T(8,128)(2,1)} %param.5), kind=kLoop, calls=%fused_computation.31 | loop fusion | flops 4194304 | bytes 25165824 | tf_op jit(solution)/shard_map/convert_element_type | solution.py:47
  19.4 0.0 reduce-scatter.2.cloned.1.call-update
  19.5 0.0 all-reduce.4.cloned.1.call-start
  20.2 86.7 %all-gather.6.cloned.1.call-done = f32[8,1,256,1024]{3,2,1,0:T(8,128)} async-done(((f32[1,1,256,1024]{3,2,1,0:T(8,128)}), f32[8,1,256,1024]{3,2,1,0:T(8,128)}) %all-gather.6.cloned.1.call-update) | async-done | bytes 8388624 | tf_op jit(solution)/shard_map/all_gather | solution.py:57
  107.0 0.3 conditional.1
  107.0 0.3 broadcast.240
  107.2 2.3 broadcast_select_fusion.1
  109.5 0.0 all-reduce.4.cloned.1.call-update
  109.5 0.0 all-gather.4.cloned.1.call-start
  109.5 418.0 %reduce-scatter.2.cloned.1.call-done = f32[1,128,1024]{2,1,0:T(8,128)} async-done(((f32[32,128,1024]{2,1,0:T(8,128)}), f32[1,128,1024]{2,1,0:T(8,128)}) %reduce-scatter.2.cloned.1.call-update) | async-done | bytes 524304 | tf_op jit(solution)/shard_map/reduce_scatter | solution.py:46
  527.5 2.4 multiply_reduce_fusion.2
  530.0 0.0 all-gather.4.cloned.1.call-update
  530.0 0.0 all-reduce.4.cloned.1.call-done
  530.0 67.0 %all-gather.4.cloned.1.call-done = bf16[1,1024,1024]{2,1,0:T(8,128)(2,1)} async-done(((bf16[1,128,1024]{2,1,0:T(8,128)(2,1)}), bf16[1,1024,1024]{2,1,0:T(8,128)(2,1)}) %all-gather.4.cloned.1.call-update) | async-done | bytes 2097168 | tf_op jit(solution)/shard_map/all_gather | solution.py:65
  597.1 3.7 multiply_reduce_fusion.1
  600.8 16.6 %all-reduce = (f32[]{:T(128)}, f32[]{:T(128)}) all-reduce(f32[]{:T(128)} %get-tuple-element.250, f32[]{:T(128)} %get-tuple-element.256), channel_id=1, replica_groups=mesh['dp'=32,'owner'=8] {'owner'}, use_global_device_ids=true, to_apply=%region_7.8 | all-reduce | flops 2 | bytes 16 | tf_op jit(solution)/shard_map/psum | solution.py:70
  618.6 0.8 multiply_bitcast_fusion
  (2 shorter events, 0.0 us)
Async XLA Ops:
  7.4 99.6 %all-gather.6.cloned.1.call-start = ((), (), s32[]{:S(2)}) async-start(), calls=%async_computation.3 | async-start | bytes 9437184 | tf_op jit(solution)/shard_map/all_gather | solution.py:57
  8.1 519.5 %reduce-scatter.2.cloned.1.call-start = ((), (), s32[]{:S(2)}) async-start(), calls=%async_computation.1 | async-start | bytes 17301504 | tf_op jit(solution)/shard_map/reduce_scatter | solution.py:46
  19.5 510.6 %all-reduce.4.cloned.1.call-start = ((), (), s32[]{:S(2)}) async-start(), calls=%async_computation.4 | async-start | bytes 8388608 | tf_op jit(solution)/shard_map/psum | solution.py:9
  109.5 487.6 %all-gather.4.cloned.1.call-start = ((), (), s32[]{:S(2)}) async-start(), calls=%async_computation.2 | async-start | bytes 2359296 | tf_op jit(solution)/shard_map/all_gather | solution.py:65
Sparse Core Ops, SparseCore 0:
  10.0 96.9 all-gather.5
  109.7 302.6 all-reduce.3
  530.1 66.9 all-gather.3
Sparse Core Ops, SparseCore 1:
  19.5 507.9 reduce-scatter.1
where the time goes:
time: 627 us
  waiting for transfers between devices  573 us (91%)
  other arithmetic  16.8 us (3%)
  blocking collectives  16.6 us (3%)
  between operations  16.6 us (3%)
    reduce_scatter x1, waiting for transfers between devices, local(): lax.psum_scatter(grad_partial[0].astype(jnp.float32), 'dp', scatter_dimen...  418 us
    all_gather x1, waiting for transfers between devices, local(): every_stats = lax.all_gather(factor_stats[0], 'owner', axis=0, tiled=True)  86.7 us
    all_gather x1, waiting for transfers between devices, local(): lax.all_gather(grad_rows_bf, 'owner', axis=1, tiled=True)[0]  67 us
    psum x1, blocking collectives, local(): lax.psum((jnp.sum(grad_wide * grad_wide), jnp.sum(precond * precond)), 'o...  16.6 us
  transfers between devices with their start and end apart: 4, of which 3 were waited for; matrix products, arithmetic and copies ran while one was open for 3% of the time, Pallas kernels for 0%

commit v1 on v0

v1 whole, which is shorter than its diff:
```python
import functools

import jax
import jax.numpy as jnp
from jax import lax
from jax.experimental import pallas as pl
from jax.experimental.pallas import tpu as pltpu
from jax.sharding import Mesh
from jax.sharding import PartitionSpec as P

FINE = ("zh", "y", "x", "zl", "c")


def fine_mesh(mesh):
    return Mesh(mesh.devices.reshape(2, 4, 4, 4, 2), FINE)


def shift(array, axis, step):
    size = lax.axis_size(axis)
    return lax.ppermute(array, axis, [(i, (i + step) % size) for i in range(size)])


def swap(array, axis, mask):
    size = lax.axis_size(axis)
    return lax.ppermute(array, axis, [(i, i ^ mask) for i in range(size)])


def f32sum(*terms):
    total = terms[0].astype(jnp.float32)
    for term in terms[1:]:
        total = total + term.astype(jnp.float32)
    return total


def narrow(*terms):
    return f32sum(*terms).astype(jnp.bfloat16)


VMEM = pl.BlockSpec(memory_space=pltpu.VMEM)
SMEM = pl.BlockSpec(memory_space=pltpu.SMEM)
HBM = pl.BlockSpec(memory_space=pltpu.HBM)


def call(kernel, name, out_shape, in_specs, operands, scratch=(), mib=16, flops=0, moved=0):
    outs = (VMEM,) * len(out_shape) if isinstance(out_shape, tuple) else VMEM
    return pl.pallas_call(
        kernel,
        out_shape=out_shape,
        in_specs=in_specs,
        out_specs=outs,
        scratch_shapes=list(scratch),
        compiler_params=pltpu.CompilerParams(vmem_limit_bytes=mib * 2**20),
        cost_estimate=pl.CostEstimate(flops=flops, bytes_accessed=moved, transcendentals=0),
        name=name,
    )(*operands)


def ring_first(up, down, axis):
    return shift(up, axis, 1), shift(down, axis, -1)


def pass_kernel(mid_ref, up_ref, down_ref, last_up_ref, last_down_ref):
    count, rows, _ = last_up_ref.shape
    for block in range(count):
        for row in range(0, rows, 32):
            at = pl.ds(row, 32)
            last_up_ref[block, at] = narrow(mid_ref[block, at], up_ref[block, at])
            last_down_ref[block, at] = narrow(mid_ref[count + block, at], down_ref[block, at])


def ring_second(mid, up, down, axis):
    count = mid.shape[0] // 2
    last = jax.ShapeDtypeStruct((count,) + mid.shape[1:], mid.dtype)
    last_up, last_down = call(
        pass_kernel, "pass_on", (last, last), [VMEM] * 3, (mid, up, down), flops=mid.size, moved=6 * mid.size
    )
    return shift(last_up, axis, 1), shift(last_down, axis, -1)


def turn_kernel(place_ref, own_ref, up_ref, down_ref, last_up_ref, last_down_ref, next_up, next_down, next_mid, next_own, sum_ref):
    rows = own_ref.shape[1]
    half = rows // 2
    for block in range(2):
        for row in range(0, rows, 32):
            at = pl.ds(row, 32)
            sum_ref[block, at] = narrow(own_ref[block, at], last_up_ref[block, at], down_ref[2 + block, at])
            sum_ref[2 + block, at] = narrow(own_ref[2 + block, at], up_ref[2 + block, at], last_down_ref[block, at])
    low, high = pl.ds(0, half), pl.ds(half, half)
    here = place_ref[0]
    ahead, across, behind = (lax.rem(here + step, 4) for step in (1, 2, 3))
    next_up[0] = sum_ref[across, low]
    next_up[1] = sum_ref[ahead, high]
    next_down[0] = sum_ref[across, high]
    next_down[1] = sum_ref[behind, low]
    next_mid[0] = sum_ref[ahead, low]
    next_mid[1] = sum_ref[behind, high]
    next_own[0] = sum_ref[here, low]
    next_own[1] = sum_ref[here, high]


def turn(place, own, up, down, last_up, last_down):
    rows, size = own.shape[1:]
    part = jax.ShapeDtypeStruct((2, rows // 2, size), own.dtype)
    return call(
        turn_kernel,
        "turn",
        (part,) * 4,
        [SMEM] + [VMEM] * 5,
        (place, own, up, down, last_up, last_down),
        scratch=[pltpu.VMEM(own.shape, own.dtype)],
        flops=2 * own.size,
        moved=8 * own.size,
    )


def pieces_kernel(*refs):
    out_ref = refs[-1]
    width = out_ref.shape[2]
    for side in range(2):
        own, up, down, last_up, last_down = refs[5 * side : 5 * side + 5]
        half = own.shape[1]
        for row in range(0, half, 32):
            at = pl.ds(row, 32)
            low = narrow(own[0, at], last_up[0, at], down[1, at])
            high = narrow(own[1, at], up[1, at], last_down[0, at])
            for piece in range(8):
                columns = slice(piece * width, (piece + 1) * width)
                out_ref[8 * side + piece, at] = low[:, columns]
                out_ref[8 * side + piece, pl.ds(half + row, 32)] = high[:, columns]


def make_pieces(*parts):
    rows, size = 2 * parts[0].shape[1], parts[0].shape[2]
    out = jax.ShapeDtypeStruct((16, rows, size // 8), jnp.bfloat16)
    return call(
        pieces_kernel, "pieces", out, [VMEM] * 10, parts, flops=4 * rows * size, moved=16 * rows * size
    )


def begin_blocks(grads_ref, moves, sems):
    copies = [
        pltpu.make_async_copy(grads_ref.at[where], out.at[slot], sems.at[i])
        for i, (where, out, slot) in enumerate(moves)
    ]
    for each in copies:
        each.start()
    return copies


def steps(place_ref, which):
    return tuple(lax.rem(place_ref[which] + step, 4) for step in range(4))


def send_kernel(place_ref, grads_ref, stats_ref, x_up, x_down, y_up, y_down, narrow_ref, sems, wide_ref):
    x, y = steps(place_ref, 0), steps(place_ref, 1)
    moves = []
    for i in range(2):
        moves += [
            ((0, i, x[2]), x_up, i),
            ((0, 2 + i, x[1]), x_up, 2 + i),
            ((0, 2 + i, x[2]), x_down, i),
            ((0, i, x[3]), x_down, 2 + i),
            ((1, y[2], i), y_up, i),
            ((1, y[1], 2 + i), y_up, 2 + i),
            ((1, y[2], 2 + i), y_down, i),
            ((1, y[3], i), y_down, 2 + i),
        ]
    stats_copy = pltpu.make_async_copy(stats_ref, wide_ref, sems.at[16])
    stats_copy.start()
    copies = begin_blocks(grads_ref, moves, sems)
    stats_copy.wait()
    for row in range(0, wide_ref.shape[0], 32):
        at = pl.ds(row, 32)
        narrow_ref[at] = wide_ref[at].astype(jnp.bfloat16)
    for each in copies:
        each.wait()


def keep_kernel(place_ref, grads_ref, x_mid, x_own, y_mid, y_own, sems):
    x, y = steps(place_ref, 0), steps(place_ref, 1)
    moves = []
    for i in range(2):
        moves += [
            ((0, i, x[1]), x_mid, i),
            ((0, 2 + i, x[3]), x_mid, 2 + i),
            ((1, y[1], i), y_mid, i),
            ((1, y[3], 2 + i), y_mid, 2 + i),
        ]
    for i in range(4):
        moves += [((0, i, x[0]), x_own, i), ((1, y[0], i), y_own, i)]
    for each in begin_blocks(grads_ref, moves, sems):
        each.wait()


def pack(kernel, place, grads, stats=None):
    mib = 16 if stats is None else 48
    outs = (jax.ShapeDtypeStruct((4,) + grads.shape[3:], grads.dtype),) * 4
    specs, operands = [SMEM, HBM], (place, grads)
    scratch = [pltpu.SemaphoreType.DMA((17,))]
    if stats is not None:
        outs += (jax.ShapeDtypeStruct(stats.shape, jnp.bfloat16),)
        specs, operands = specs + [HBM], operands + (stats,)
        scratch += [pltpu.VMEM(stats.shape, stats.dtype)]
    return call(kernel, kernel.__name__[:4], outs, specs, operands, scratch=scratch, mib=mib, moved=2**23)


def root_kernel(side, offset_ref, stats_ref, out_ref, start_ref, first_ref, second_ref, third_ref):
    size = out_ref.shape[0]
    slot = size // 4

    def eye_rows(tile):
        row_ids = lax.broadcasted_iota(jnp.int32, (slot, size), 0) + tile * slot
        col_ids = lax.broadcasted_iota(jnp.int32, (slot, size), 1)
        return jnp.where(row_ids == col_ids, 1.0, 0.0).astype(jnp.float32)

    def rows(tile):
        return pl.ds(tile * slot, slot)

    def held(tile):
        at = lax.rem(offset_ref[0] + side * 4 + tile, 8)
        return stats_ref[pl.ds(pl.multiple_of(at * slot, slot), slot), :].astype(jnp.float32)

    total = jnp.zeros((1, size), jnp.float32)
    for tile in range(4):
        values = held(tile)
        total = total + jnp.sum(values * values, axis=0, keepdims=True)
    inverse = 1.0 / jnp.sqrt(jnp.sum(total))

    for tile in range(4):
        normed = held(tile) * inverse
        start_ref[rows(tile), :] = normed.astype(jnp.bfloat16)
        first_ref[rows(tile), :] = (1.5 * eye_rows(tile) - 0.5 * normed).astype(jnp.bfloat16)
    for tile in range(4):
        product = jnp.dot(start_ref[rows(tile), :], first_ref[...], preferred_element_type=jnp.float32)
        second_ref[rows(tile), :] = product.astype(jnp.bfloat16)
    for tile in range(4):
        product = jnp.dot(first_ref[rows(tile), :], second_ref[...], preferred_element_type=jnp.float32)
        third_ref[rows(tile), :] = (1.5 * eye_rows(tile) - 0.5 * product).astype(jnp.bfloat16)
    for tile in range(4):
        product = jnp.dot(third_ref[rows(tile), :], first_ref[...], preferred_element_type=jnp.float32)
        out_ref[rows(tile), :] = product.astype(jnp.bfloat16)


def inverse_root(side, stats, offset):
    size = stats.shape[1]
    return call(
        functools.partial(root_kernel, side),
        ("left_root", "right_root")[side],
        jax.ShapeDtypeStruct((size, size), jnp.bfloat16),
        [SMEM, VMEM],
        (offset, stats),
        scratch=[pltpu.VMEM((size, size), jnp.bfloat16)] * 4,
        mib=24,
        flops=6 * size**3,
        moved=4 * size * size,
    )


def lanes(squares):
    rows, columns = squares.shape
    total = jnp.sum(squares.reshape(rows // 8, 8, columns), axis=0)
    return sum(total[:, at : at + 128] for at in range(0, columns, 128))


def mix_kernel(pieces_ref, left_ref, out_ref, energy_ref, grad_ref):
    count, rows, _ = out_ref.shape
    energy = jnp.zeros(energy_ref.shape, jnp.float32)
    for piece in range(count):
        grad = narrow(pieces_ref[piece], pieces_ref[count + piece])
        grad_ref[pl.ds(piece * rows, rows), :] = grad
        wide = grad.astype(jnp.float32)
        energy = energy + lanes(wide * wide)
    energy_ref[...] = energy
    for piece in range(0, count, 2):
        product = jnp.dot(
            left_ref[pl.ds(piece * rows, 2 * rows), :], grad_ref[...], preferred_element_type=jnp.float32
        ).astype(jnp.bfloat16)
        out_ref[piece] = product[:rows]
        out_ref[piece + 1] = product[rows:]


def mix(pieces, left_root):
    _, rows, width = pieces.shape
    return call(
        mix_kernel,
        "mix",
        (jax.ShapeDtypeStruct((8, rows, width), jnp.bfloat16), jax.ShapeDtypeStruct((8, 128), jnp.float32)),
        [VMEM] * 2,
        (pieces, left_root),
        scratch=[pltpu.VMEM((8 * rows, width), jnp.bfloat16)],
        flops=2 * left_root.size * width,
        moved=2 * left_root.size,
    )


def condition_kernel(mixed_ref, right_ref, energy_ref, out_ref, totals_ref, rows_ref):
    count, _, width = mixed_ref.shape
    for piece in range(count):
        rows_ref[:, pl.ds(piece * width, width)] = mixed_ref[piece]
    total = jnp.zeros(energy_ref.shape, jnp.float32)
    for at in range(0, out_ref.shape[1], 256):
        product = jnp.dot(rows_ref[...], right_ref[:, pl.ds(at, 256)], preferred_element_type=jnp.float32)
        out_ref[:, pl.ds(at, 256)] = product
        total = total + lanes(product * product)
    totals_ref[:8] = energy_ref[...]
    totals_ref[8:] = total


def condition(mixed, right_root, energy):
    _, rows, width = mixed.shape
    size = right_root.shape[1]
    return call(
        condition_kernel,
        "condition",
        (jax.ShapeDtypeStruct((rows, size), jnp.float32), jax.ShapeDtypeStruct((16, 128), jnp.float32)),
        [VMEM] * 3,
        (mixed, right_root, energy),
        scratch=[pltpu.VMEM((rows, size), jnp.bfloat16)],
        flops=2 * rows * right_root.size,
        moved=2 * right_root.size,
    )


def finish_kernel(count, totals_ref, precond_ref, out_ref):
    grad_mean = jnp.sum(totals_ref[:8]) / count
    cond_mean = jnp.sum(totals_ref[8:]) / count
    factor = jnp.sqrt(grad_mean / (cond_mean + 1e-06))
    for row in range(0, out_ref.shape[0], 32):
        at = pl.ds(row, 32)
        out_ref[at] = precond_ref[at] * factor


def finish(totals, precond, count):
    return call(
        functools.partial(finish_kernel, count),
        "finish",
        jax.ShapeDtypeStruct(precond.shape, jnp.float32),
        [VMEM] * 2,
        (totals, precond),
        flops=precond.size,
        moved=8 * precond.size,
    )


def local(grad_partial, factor_stats, owner_table):
    size = grad_partial.shape[3]
    rows_here = grad_partial.shape[2]
    owner = ("zl", "c")
    grads = grad_partial.reshape(2, 4, 4, rows_here, size)
    x, y = lax.axis_index("x").astype(jnp.int32), lax.axis_index("y").astype(jnp.int32)
    place = jnp.stack((x, y))

    x_up, x_down, y_up, y_down, own = pack(send_kernel, place, grads, factor_stats[0, 0])
    place, x_up, own = lax.optimization_barrier((place, x_up, own))
    stats = lax.all_gather(own, owner, axis=0, tiled=True)
    x_ends = ring_first(x_up, x_down, "x")
    y_ends = ring_first(y_up, y_down, "y")
    x_mid, x_own, y_mid, y_own = pack(keep_kernel, place, grads)

    x_last = ring_second(x_mid, *x_ends, "x")
    y_last = ring_second(y_mid, *y_ends, "y")
    lower_up, lower_down, lower_mid, lower_own = turn(y[None], x_own, *x_ends, *x_last)
    lower_ends = ring_first(lower_up, lower_down, "y")
    upper_up, upper_down, upper_mid, upper_own = turn(x[None], y_own, *y_ends, *y_last)
    upper_ends = ring_first(upper_up, upper_down, "x")
    lower_last = ring_second(lower_mid, *lower_ends, "y")
    upper_last = ring_second(upper_mid, *upper_ends, "x")
    pieces = make_pieces(lower_own, *lower_ends, *lower_last, upper_own, *upper_ends, *upper_last)
    pieces, stats = lax.optimization_barrier((pieces, stats))
    pieces = lax.all_to_all(pieces, ("zh",) + owner, split_axis=0, concat_axis=0, tiled=True)
    left_root = inverse_root(0, stats, owner_table)
    right_root = inverse_root(1, stats, owner_table)

    mixed, energy = mix(pieces, left_root)
    mixed, right_root = lax.optimization_barrier((mixed, right_root))
    mixed = lax.all_to_all(mixed, owner, split_axis=0, concat_axis=0, tiled=True)
    precond, totals = condition(mixed, right_root, energy)
    totals = totals + swap(totals, "c", 1)
    totals = totals + swap(totals, "zl", 1)
    totals = totals + swap(totals, "zl", 2)
    return finish(totals, precond, float(size * size))[None]


def solution(mesh):
    dp, owner = ("zh", "y", "x"), ("zl", "c")
    placed = (P(dp, None, owner, None), P(dp, owner, None, None), P(dp))
    return jax.shard_map(
        local, mesh=fine_mesh(mesh), in_specs=placed, out_specs=P(dp, owner, None), check_vma=False
    )
```

time: 627 us -> 134 us (0.21)
  waiting for transfers between devices: 573 us -> 39.3 us
  starting transfers between devices: 0.13 us -> 31.2 us
  Pallas kernels: 0 us -> 24.6 us
  other arithmetic: 16.8 us -> 0.08 us
  local copies, waits for them, and re-layouts: 0.25 us -> 9.15 us
    reduce_scatter x1 -> x0, waiting for transfers between devices: 418 us -> none  [local(): lax.psum_scatter(grad_partial[0].astype(jnp.float32), 'dp', scatter_dimen...]
    all_gather x2 -> x1, waiting for transfers between devices: 154 us -> 0.01 us  [local(): stats = lax.all_gather(own, owner, axis=0, tiled=True)]
    ppermute x0 -> x19, waiting for transfers between devices: none -> 39.3 us  [the longest x16 30.1 us: shift(): lax.ppermute(array, axis, [(i, (i + step) % size) for i in range(size)])]
    pallas_call x0 -> x14, Pallas kernels: none -> 24.6 us  [call(): pl.pallas_call(kernel, out_shape=out_shape, in_specs=in_specs, out_specs=...]
    ppermute x0 -> x19, starting transfers between devices: none -> 22.3 us  [the longest x16 22 us: shift(): lax.ppermute(array, axis, [(i, (i + step) % size) for i in range(size)])]
    psum x1 -> x0, blocking collectives: 16.6 us -> none  [local(): lax.psum((jnp.sum(grad_wide * grad_wide), jnp.sum(precond * precond)), 'o...]
    all_to_all x0 -> x1, blocking collectives: none -> 14.3 us  [local(): lax.all_to_all(mixed, owner, split_axis=0, concat_axis=0, tiled=True)]
    convert_element_type x1 -> x0, other arithmetic: 11.3 us -> none  [local(): grad_partial[0].astype(jnp.float32)]
  transfers between devices with their start and end apart: 4 -> 21, of which waited for: 3 -> 10; matrix products, arithmetic and copies ran while one was open for 3% -> 0% of each run, Pallas kernels for 0% -> 14%
where the time goes in v1:
time: 134 us; the launch traced here: 133 us
  waiting for transfers between devices  39.3 us (29%)
  starting transfers between devices  31.2 us (23%)
  Pallas kernels  24.6 us (18%)
  blocking collectives  14.3 us (11%)
  between operations  14.2 us (11%)
  local copies, waits for them, and re-layouts  9.15 us (7%)
    ppermute x16, waiting for transfers between devices, shift(): lax.ppermute(array, axis, [(i, (i + step) % size) for i in range(size)])  30.1 us
    pallas_call x14, Pallas kernels, call(): pl.pallas_call(kernel, out_shape=out_shape, in_specs=in_specs, out_specs=...  24.6 us
    ppermute x16, starting transfers between devices, shift(): lax.ppermute(array, axis, [(i, (i + step) % size) for i in range(size)])  22 us
    all_to_all x1, blocking collectives, local(): lax.all_to_all(mixed, owner, split_axis=0, concat_axis=0, tiled=True)  14.3 us
    ppermute x3, waiting for transfers between devices, swap(): return lax.ppermute(array, axis, [(i, i ^ mask) for i in range(size)])  9.19 us
    unnamed x12, local copies, waits for them, and re-layouts  9.15 us
    all_to_all x1, starting transfers between devices, local(): lax.all_to_all(pieces, ('zh',) + owner, split_axis=0, concat_axis=0, tile...  8.9 us
  transfers between devices with their start and end apart: 21, of which 10 were waited for; matrix products, arithmetic and copies ran while one was open for 0% of the time, Pallas kernels for 14%

profile of v1, /device:TPU:6, one launch (start us, length us, event | category | flops | bytes accessed | tf_op | source)
XLA Modules:
  0.0 132.9 jit_solution(16367000832896984570)
XLA Ops:
  6.6 1.2 copy-done.3
  7.8 3.7 %send.1 = (bf16[4,128,1024]{2,1,0:T(8,128)(2,1)S(1)}, bf16[4,128,1024]{2,1,0:T(8,128)(2,1)S(1)}, bf16[4,128,1024]{2,1,0:T(8,128)(2,1)S(1)}, bf16[4,128,1024]{2,1,0:T(8,128)(2,1)S(1)}, bf16[256,1024]{1,0:T(8,128)(2,1)}) custom-call(s32[2]{0:T(128)S(1)} %pad_add_fusion.place_ref, bf16[2,4,4,128,1024]{4,3,2,1,0:T(8,128)(2,1)} %bitcast.5, f32[256,1024]{1,0:T(8,128)S(1)} %bitcast.7), custom_call_target="tpu_custom_call" | custom-call | bytes 8388608 | tf_op jit(solution)/shard_map/send/pallas_call | solution.py:46
  11.6 1.0 copy-done.5
  12.6 1.7 %collective-permute-start.8 = (bf16[4,128,1024]{2,1,0:T(8,128)(2,1)}, bf16[4,128,1024]{2,1,0:T(8,128)(2,1)S(1)}, u32[]{:S(2)}, u32[]{:S(2)}) collective-permute-start(bf16[4,128,1024]{2,1,0:T(8,128)(2,1)} %copy-done.5), channel_id=1, source_target_pairs={{0,32},{32,64},{64,96},{96,0},{1,33},{33,65},{65,97},{97,1},{2,34}... | collective-permute-start | bytes 3145736 | tf_op jit(solution)/shard_map/ppermute | solution.py:20
  14.2 1.7 %collective-permute-start.9 = (bf16[4,128,1024]{2,1,0:T(8,128)(2,1)S(1)}, bf16[4,128,1024]{2,1,0:T(8,128)(2,1)S(1)}, u32[]{:S(2)}, u32[]{:S(2)}) collective-permute-start(bf16[4,128,1024]{2,1,0:T(8,128)(2,1)S(1)} %get-tuple-element.58), channel_id=1, source_target_pairs={{0,96},{32,0},{64,32},{96,64},{1,97},{33,1},{65,33},{97,65},{2,98}... | collective-permute-start | bytes 3145736 | tf_op jit(solution)/shard_map/ppermute | solution.py:20
  15.9 2.2 %collective-permute-start = (bf16[4,128,1024]{2,1,0:T(8,128)(2,1)S(1)}, bf16[4,128,1024]{2,1,0:T(8,128)(2,1)S(1)}, u32[]{:S(2)}, u32[]{:S(2)}) collective-permute-start(bf16[4,128,1024]{2,1,0:T(8,128)(2,1)S(1)} %get-tuple-element.45), channel_id=1, source_target_pairs={{0,8},{8,16},{16,24},{24,0},{1,9},{9,17},{17,25},{25,1},{2,10},{10... | collective-permute-start | bytes 3145736 | tf_op jit(solution)/shard_map/ppermute | solution.py:20
  18.1 3.4 %copy-done = bf16[1,32,128,1024]{3,2,1,0:T(8,128)(2,1)S(1)} copy-done((bf16[1,32,128,1024]{3,2,1,0:T(8,128)(2,1)S(1)}, bf16[1,32,128,1024]{3,2,1,0:T(8,128)(2,1)}, u32[]{:S(2)}) %copy-start) | copy-done | bytes 8388632
  21.5 1.0 keep.1
  22.5 16.5 %collective-permute-done.8.up_ref = bf16[4,128,1024]{2,1,0:T(8,128)(2,1)S(1)} collective-permute-done((bf16[4,128,1024]{2,1,0:T(8,128)(2,1)}, bf16[4,128,1024]{2,1,0:T(8,128)(2,1)S(1)}, u32[]{:S(2)}, u32[]{:S(2)}) %collective-permute-start.8) | collective-permute-done | bytes 1048608 | tf_op jit(solution)/shard_map/ppermute | solution.py:20
  39.3 1.5 %collective-permute-start.10 = (bf16[2,128,1024]{2,1,0:T(8,128)(2,1)S(1)}, bf16[2,128,1024]{2,1,0:T(8,128)(2,1)S(1)}, u32[]{:S(2)}, u32[]{:S(2)}) collective-permute-start(bf16[2,128,1024]{2,1,0:T(8,128)(2,1)S(1)} %get-tuple-element.60), channel_id=1, source_target_pairs={{0,32},{32,64},{64,96},{96,0},{1,33},{33,65},{65,97},{97,1},{2,34}... | collective-permute-start | bytes 1572872 | tf_op jit(solution)/shard_map/ppermute | solution.py:20
  40.8 1.9 %collective-permute-start.11 = (bf16[2,128,1024]{2,1,0:T(8,128)(2,1)S(1)}, bf16[2,128,1024]{2,1,0:T(8,128)(2,1)S(1)}, u32[]{:S(2)}, u32[]{:S(2)}) collective-permute-start(bf16[2,128,1024]{2,1,0:T(8,128)(2,1)S(1)} %get-tuple-element.61), channel_id=1, source_target_pairs={{0,96},{32,0},{64,32},{96,64},{1,97},{33,1},{65,33},{97,65},{2,98}... | collective-permute-start | bytes 1572872 | tf_op jit(solution)/shard_map/ppermute | solution.py:20
  43.4 1.5 %collective-permute-start.3 = (bf16[2,128,1024]{2,1,0:T(8,128)(2,1)S(1)}, bf16[2,128,1024]{2,1,0:T(8,128)(2,1)S(1)}, u32[]{:S(2)}, u32[]{:S(2)}) collective-permute-start(bf16[2,128,1024]{2,1,0:T(8,128)(2,1)S(1)} %get-tuple-element.49), channel_id=1, source_target_pairs={{0,24},{8,0},{16,8},{24,16},{1,25},{9,1},{17,9},{25,17},{2,26},{10... | collective-permute-start | bytes 1572872 | tf_op jit(solution)/shard_map/ppermute | solution.py:20
  45.0 8.6 %collective-permute-done.10.last_up_ref = bf16[2,128,1024]{2,1,0:T(8,128)(2,1)S(1)} collective-permute-done((bf16[2,128,1024]{2,1,0:T(8,128)(2,1)S(1)}, bf16[2,128,1024]{2,1,0:T(8,128)(2,1)S(1)}, u32[]{:S(2)}, u32[]{:S(2)}) %collective-permute-start.10) | collective-permute-done | bytes 524320 | tf_op jit(solution)/shard_map/ppermute | solution.py:20
  54.1 2.0 %collective-permute-start.13 = (bf16[2,64,1024]{2,1,0:T(8,128)(2,1)S(1)}, bf16[2,64,1024]{2,1,0:T(8,128)(2,1)S(1)}, u32[]{:S(2)}, u32[]{:S(2)}) collective-permute-start(bf16[2,64,1024]{2,1,0:T(8,128)(2,1)S(1)} %get-tuple-element.64), channel_id=1, source_target_pairs={{0,24},{8,0},{16,8},{24,16},{1,25},{9,1},{17,9},{25,17},{2,26},{10... | collective-permute-start | bytes 786440 | tf_op jit(solution)/shard_map/ppermute | solution.py:20
  56.1 0.8 collective-permute-done.3.last_down_ref
  57.5 3.2 %collective-permute-start.5 = (bf16[2,64,1024]{2,1,0:T(8,128)(2,1)S(1)}, bf16[2,64,1024]{2,1,0:T(8,128)(2,1)S(1)}, u32[]{:S(2)}, u32[]{:S(2)}) collective-permute-start(bf16[2,64,1024]{2,1,0:T(8,128)(2,1)S(1)} %get-tuple-element.52), channel_id=1, source_target_pairs={{0,96},{32,0},{64,32},{96,64},{1,97},{33,1},{65,33},{97,65},{2,98}... | collective-permute-start | bytes 786440 | tf_op jit(solution)/shard_map/ppermute | solution.py:20
  61.0 1.3 collective-permute-done.13.down_ref.refs_7_
  63.0 1.6 %collective-permute-start.15 = (bf16[1,64,1024]{2,1,0:T(8,128)(2,1)S(1)}, bf16[1,64,1024]{2,1,0:T(8,128)(2,1)S(1)}, u32[]{:S(2)}, u32[]{:S(2)}) collective-permute-start(bf16[1,64,1024]{2,1,0:T(8,128)(2,1)S(1)} %get-tuple-element.67), channel_id=1, source_target_pairs={{0,24},{8,0},{16,8},{24,16},{1,25},{9,1},{17,9},{25,17},{2,26},{10... | collective-permute-start | bytes 393224 | tf_op jit(solution)/shard_map/ppermute | solution.py:20
  65.7 2.8 %collective-permute-start.7 = (bf16[1,64,1024]{2,1,0:T(8,128)(2,1)S(1)}, bf16[1,64,1024]{2,1,0:T(8,128)(2,1)S(1)}, u32[]{:S(2)}, u32[]{:S(2)}) collective-permute-start(bf16[1,64,1024]{2,1,0:T(8,128)(2,1)S(1)} %get-tuple-element.55), channel_id=1, source_target_pairs={{0,96},{32,0},{64,32},{96,64},{1,97},{33,1},{65,33},{97,65},{2,98}... | collective-permute-start | bytes 393224 | tf_op jit(solution)/shard_map/ppermute | solution.py:20
  69.2 2.2 %collective-permute-done.6.refs_3_ = bf16[1,64,1024]{2,1,0:T(8,128)(2,1)S(1)} collective-permute-done((bf16[1,64,1024]{2,1,0:T(8,128)(2,1)S(1)}, bf16[1,64,1024]{2,1,0:T(8,128)(2,1)S(1)}, u32[]{:S(2)}, u32[]{:S(2)}) %collective-permute-start.6) | collective-permute-done | bytes 131104 | tf_op jit(solution)/shard_map/ppermute | solution.py:20
  71.4 1.0 pieces.1
  72.4 8.9 %all-to-all-start = ((bf16[16,128,128]{2,1,0:T(8,128)(2,1)}), bf16[16,128,128]{2,1,0:T(8,128)(2,1)S(1)}, u32[]{:S(2)}, u32[]{:S(2)}) async-start(bf16[16,128,128]{2,1,0:T(8,128)(2,1)} %pieces.1), calls=%async_computation | async-start | bytes 1048576 | tf_op jit(solution)/shard_map/all_to_all | solution.py:370
  81.3 2.2 %copy-done.4 = bf16[2048,1024]{1,0:T(8,128)(2,1)S(1)} copy-done((bf16[2048,1024]{1,0:T(8,128)(2,1)S(1)}, bf16[2048,1024]{1,0:T(8,128)(2,1)}, u32[]{:S(2)}) %copy-start.4) | copy-done | bytes 4194328
  83.5 7.4 %left_root.1.left_ref = bf16[1024,1024]{1,0:T(8,128)(2,1)S(1)} custom-call(s32[1]{0:T(128)S(6)} %copy.4.offset_ref, bf16[2048,1024]{1,0:T(8,128)(2,1)S(1)} %copy-done.4), custom_call_target="tpu_custom_call" | custom-call | flops 6442450944 | bytes 4194304 | tf_op jit(solution)/shard_map/left_root/pallas_call | solution.py:46
  90.9 7.7 %right_root.1.right_ref = bf16[1024,1024]{1,0:T(8,128)(2,1)S(1)} custom-call(s32[1]{0:T(128)S(6)} %copy.4.offset_ref, bf16[2048,1024]{1,0:T(8,128)(2,1)S(1)} %copy-done.4), custom_call_target="tpu_custom_call" | custom-call | flops 6442450944 | bytes 4194304 | tf_op jit(solution)/shard_map/right_root/pallas_call | solution.py:46
  98.5 1.4 %copy-done.1 = bf16[1024,1024]{1,0:T(8,128)(2,1)} copy-done((bf16[1024,1024]{1,0:T(8,128)(2,1)}, bf16[1024,1024]{1,0:T(8,128)(2,1)S(1)}, u32[]{:S(2)}) %copy-start.1) | copy-done | bytes 2097176
  99.9 0.8 mix.1
  100.7 14.3 %all_to_all.10.mixed_ref = bf16[8,128,128]{2,1,0:T(8,128)(2,1)S(1)} all-to-all(bf16[8,128,128]{2,1,0:T(8,128)(2,1)S(1)} %get-tuple-element.72), channel_id=1, replica_groups=mesh['zh'=2,'y'=4,'x'=4,'zl'=4,'c'=2] {'zl','c'}, dimensions={0} | all-to-all | bytes 524288 | tf_op jit(solution)/shard_map/all_to_all | solution.py:376
  115.6 1.2 collective-permute-done.16
  116.9 3.5 %collective-permute-done.17 = f32[16,128]{1,0:T(8,128)S(1)} collective-permute-done((f32[16,128]{1,0:T(8,128)S(1)}, f32[16,128]{1,0:T(8,128)S(1)}, u32[]{:S(2)}, u32[]{:S(2)}) %collective-permute-start.17) | collective-permute-done | bytes 8224 | tf_op jit(solution)/shard_map/ppermute | solution.py:25
  120.4 4.5 %collective-permute-done.18 = f32[16,128]{1,0:T(8,128)S(1)} collective-permute-done((f32[16,128]{1,0:T(8,128)S(1)}, f32[16,128]{1,0:T(8,128)S(1)}, u32[]{:S(2)}, u32[]{:S(2)}) %collective-permute-start.18) | collective-permute-done | bytes 8224 | tf_op jit(solution)/shard_map/ppermute | solution.py:25
  125.0 1.0 finish.1
  (42 shorter events, 5.1 us)
Async XLA Ops:
  6.5 65.8 %all-gather.2.cloned.1.call-start = ((), (), s32[]{:S(2)}) async-start(), calls=%async_computation.2 | async-start | bytes 4718592 | tf_op jit(solution)/shard_map/all_gather | solution.py:355
  6.6 1.2 copy-start.3
  11.5 1.0 copy-start.5
  12.6 26.5 %collective-permute-start.8 = (bf16[4,128,1024]{2,1,0:T(8,128)(2,1)}, bf16[4,128,1024]{2,1,0:T(8,128)(2,1)S(1)}, u32[]{:S(2)}, u32[]{:S(2)}) collective-permute-start(bf16[4,128,1024]{2,1,0:T(8,128)(2,1)} %copy-done.5), channel_id=1, source_target_pairs={{0,32},{32,64},{64,96},{96,0},{1,33},{33,65},{65,97},{97,1},{2,34}... | collective-permute-start | bytes 3145736 | tf_op jit(solution)/shard_map/ppermute | solution.py:20
  14.2 24.8 %collective-permute-start.9 = (bf16[4,128,1024]{2,1,0:T(8,128)(2,1)S(1)}, bf16[4,128,1024]{2,1,0:T(8,128)(2,1)S(1)}, u32[]{:S(2)}, u32[]{:S(2)}) collective-permute-start(bf16[4,128,1024]{2,1,0:T(8,128)(2,1)S(1)} %get-tuple-element.58), channel_id=1, source_target_pairs={{0,96},{32,0},{64,32},{96,64},{1,97},{33,1},{65,33},{97,65},{2,98}... | collective-permute-start | bytes 3145736 | tf_op jit(solution)/shard_map/ppermute | solution.py:20
  15.9 26.7 %collective-permute-start = (bf16[4,128,1024]{2,1,0:T(8,128)(2,1)S(1)}, bf16[4,128,1024]{2,1,0:T(8,128)(2,1)S(1)}, u32[]{:S(2)}, u32[]{:S(2)}) collective-permute-start(bf16[4,128,1024]{2,1,0:T(8,128)(2,1)S(1)} %get-tuple-element.45), channel_id=1, source_target_pairs={{0,8},{8,16},{16,24},{24,0},{1,9},{9,17},{17,25},{25,1},{2,10},{10... | collective-permute-start | bytes 3145736 | tf_op jit(solution)/shard_map/ppermute | solution.py:20
  18.1 24.5 %collective-permute-start.1 = (bf16[4,128,1024]{2,1,0:T(8,128)(2,1)S(1)}, bf16[4,128,1024]{2,1,0:T(8,128)(2,1)S(1)}, u32[]{:S(2)}, u32[]{:S(2)}) collective-permute-start(bf16[4,128,1024]{2,1,0:T(8,128)(2,1)S(1)} %get-tuple-element.46), channel_id=1, source_target_pairs={{0,24},{8,0},{16,8},{24,16},{1,25},{9,1},{17,9},{25,17},{2,26},{10... | collective-permute-start | bytes 3145736 | tf_op jit(solution)/shard_map/ppermute | solution.py:20
  18.1 3.4 %copy-start = (bf16[1,32,128,1024]{3,2,1,0:T(8,128)(2,1)S(1)}, bf16[1,32,128,1024]{3,2,1,0:T(8,128)(2,1)}, u32[]{:S(2)}) copy-start(bf16[1,32,128,1024]{3,2,1,0:T(8,128)(2,1)} %param.3) | copy-start | bytes 25165828
  39.3 14.3 %collective-permute-start.10 = (bf16[2,128,1024]{2,1,0:T(8,128)(2,1)S(1)}, bf16[2,128,1024]{2,1,0:T(8,128)(2,1)S(1)}, u32[]{:S(2)}, u32[]{:S(2)}) collective-permute-start(bf16[2,128,1024]{2,1,0:T(8,128)(2,1)S(1)} %get-tuple-element.60), channel_id=1, source_target_pairs={{0,32},{32,64},{64,96},{96,0},{1,33},{33,65},{65,97},{97,1},{2,34}... | collective-permute-start | bytes 1572872 | tf_op jit(solution)/shard_map/ppermute | solution.py:20
  40.8 12.8 %collective-permute-start.11 = (bf16[2,128,1024]{2,1,0:T(8,128)(2,1)S(1)}, bf16[2,128,1024]{2,1,0:T(8,128)(2,1)S(1)}, u32[]{:S(2)}, u32[]{:S(2)}) collective-permute-start(bf16[2,128,1024]{2,1,0:T(8,128)(2,1)S(1)} %get-tuple-element.61), channel_id=1, source_target_pairs={{0,96},{32,0},{64,32},{96,64},{1,97},{33,1},{65,33},{97,65},{2,98}... | collective-permute-start | bytes 1572872 | tf_op jit(solution)/shard_map/ppermute | solution.py:20
  42.9 13.3 %collective-permute-start.2 = (bf16[2,128,1024]{2,1,0:T(8,128)(2,1)S(1)}, bf16[2,128,1024]{2,1,0:T(8,128)(2,1)S(1)}, u32[]{:S(2)}, u32[]{:S(2)}) collective-permute-start(bf16[2,128,1024]{2,1,0:T(8,128)(2,1)S(1)} %get-tuple-element.48), channel_id=1, source_target_pairs={{0,8},{8,16},{16,24},{24,0},{1,9},{9,17},{17,25},{25,1},{2,10},{10... | collective-permute-start | bytes 1572872 | tf_op jit(solution)/shard_map/ppermute | solution.py:20
  43.4 13.5 %collective-permute-start.3 = (bf16[2,128,1024]{2,1,0:T(8,128)(2,1)S(1)}, bf16[2,128,1024]{2,1,0:T(8,128)(2,1)S(1)}, u32[]{:S(2)}, u32[]{:S(2)}) collective-permute-start(bf16[2,128,1024]{2,1,0:T(8,128)(2,1)S(1)} %get-tuple-element.49), channel_id=1, source_target_pairs={{0,24},{8,0},{16,8},{24,16},{1,25},{9,1},{17,9},{25,17},{2,26},{10... | collective-permute-start | bytes 1572872 | tf_op jit(solution)/shard_map/ppermute | solution.py:20
  54.0 6.9 %collective-permute-start.12 = (bf16[2,64,1024]{2,1,0:T(8,128)(2,1)S(1)}, bf16[2,64,1024]{2,1,0:T(8,128)(2,1)S(1)}, u32[]{:S(2)}, u32[]{:S(2)}) collective-permute-start(bf16[2,64,1024]{2,1,0:T(8,128)(2,1)S(1)} %get-tuple-element.63), channel_id=1, source_target_pairs={{0,8},{8,16},{16,24},{24,0},{1,9},{9,17},{17,25},{25,1},{2,10},{10... | collective-permute-start | bytes 786440 | tf_op jit(solution)/shard_map/ppermute | solution.py:20
  54.1 8.2 %collective-permute-start.13 = (bf16[2,64,1024]{2,1,0:T(8,128)(2,1)S(1)}, bf16[2,64,1024]{2,1,0:T(8,128)(2,1)S(1)}, u32[]{:S(2)}, u32[]{:S(2)}) collective-permute-start(bf16[2,64,1024]{2,1,0:T(8,128)(2,1)S(1)} %get-tuple-element.64), channel_id=1, source_target_pairs={{0,24},{8,0},{16,8},{24,16},{1,25},{9,1},{17,9},{25,17},{2,26},{10... | collective-permute-start | bytes 786440 | tf_op jit(solution)/shard_map/ppermute | solution.py:20
  57.4 7.7 %collective-permute-start.4 = (bf16[2,64,1024]{2,1,0:T(8,128)(2,1)S(1)}, bf16[2,64,1024]{2,1,0:T(8,128)(2,1)S(1)}, u32[]{:S(2)}, u32[]{:S(2)}) collective-permute-start(bf16[2,64,1024]{2,1,0:T(8,128)(2,1)S(1)} %get-tuple-element.51), channel_id=1, source_target_pairs={{0,32},{32,64},{64,96},{96,0},{1,33},{33,65},{65,97},{97,1},{2,34}... | collective-permute-start | bytes 786440 | tf_op jit(solution)/shard_map/ppermute | solution.py:20
  57.5 7.6 %collective-permute-start.5 = (bf16[2,64,1024]{2,1,0:T(8,128)(2,1)S(1)}, bf16[2,64,1024]{2,1,0:T(8,128)(2,1)S(1)}, u32[]{:S(2)}, u32[]{:S(2)}) collective-permute-start(bf16[2,64,1024]{2,1,0:T(8,128)(2,1)S(1)} %get-tuple-element.52), channel_id=1, source_target_pairs={{0,96},{32,0},{64,32},{96,64},{1,97},{33,1},{65,33},{97,65},{2,98}... | collective-permute-start | bytes 786440 | tf_op jit(solution)/shard_map/ppermute | solution.py:20
  62.3 6.8 %collective-permute-start.14 = (bf16[1,64,1024]{2,1,0:T(8,128)(2,1)S(1)}, bf16[1,64,1024]{2,1,0:T(8,128)(2,1)S(1)}, u32[]{:S(2)}, u32[]{:S(2)}) collective-permute-start(bf16[1,64,1024]{2,1,0:T(8,128)(2,1)S(1)} %get-tuple-element.66), channel_id=1, source_target_pairs={{0,8},{8,16},{16,24},{24,0},{1,9},{9,17},{17,25},{25,1},{2,10},{10... | collective-permute-start | bytes 393224 | tf_op jit(solution)/shard_map/ppermute | solution.py:20
  63.0 6.2 %collective-permute-start.15 = (bf16[1,64,1024]{2,1,0:T(8,128)(2,1)S(1)}, bf16[1,64,1024]{2,1,0:T(8,128)(2,1)S(1)}, u32[]{:S(2)}, u32[]{:S(2)}) collective-permute-start(bf16[1,64,1024]{2,1,0:T(8,128)(2,1)S(1)} %get-tuple-element.67), channel_id=1, source_target_pairs={{0,24},{8,0},{16,8},{24,16},{1,25},{9,1},{17,9},{25,17},{2,26},{10... | collective-permute-start | bytes 393224 | tf_op jit(solution)/shard_map/ppermute | solution.py:20
  65.1 6.3 %collective-permute-start.6 = (bf16[1,64,1024]{2,1,0:T(8,128)(2,1)S(1)}, bf16[1,64,1024]{2,1,0:T(8,128)(2,1)S(1)}, u32[]{:S(2)}, u32[]{:S(2)}) collective-permute-start(bf16[1,64,1024]{2,1,0:T(8,128)(2,1)S(1)} %get-tuple-element.54), channel_id=1, source_target_pairs={{0,32},{32,64},{64,96},{96,0},{1,33},{33,65},{65,97},{97,1},{2,34}... | collective-permute-start | bytes 393224 | tf_op jit(solution)/shard_map/ppermute | solution.py:20
  65.7 5.7 %collective-permute-start.7 = (bf16[1,64,1024]{2,1,0:T(8,128)(2,1)S(1)}, bf16[1,64,1024]{2,1,0:T(8,128)(2,1)S(1)}, u32[]{:S(2)}, u32[]{:S(2)}) collective-permute-start(bf16[1,64,1024]{2,1,0:T(8,128)(2,1)S(1)} %get-tuple-element.55), channel_id=1, source_target_pairs={{0,96},{32,0},{64,32},{96,64},{1,97},{33,1},{65,33},{97,65},{2,98}... | collective-permute-start | bytes 393224 | tf_op jit(solution)/shard_map/ppermute | solution.py:20
  72.4 27.5 %all-to-all-start = ((bf16[16,128,128]{2,1,0:T(8,128)(2,1)}), bf16[16,128,128]{2,1,0:T(8,128)(2,1)S(1)}, u32[]{:S(2)}, u32[]{:S(2)}) async-start(bf16[16,128,128]{2,1,0:T(8,128)(2,1)} %pieces.1), calls=%async_computation | async-start | bytes 1048576 | tf_op jit(solution)/shard_map/all_to_all | solution.py:370
  81.3 2.2 %copy-start.4 = (bf16[2048,1024]{1,0:T(8,128)(2,1)S(1)}, bf16[2048,1024]{1,0:T(8,128)(2,1)}, u32[]{:S(2)}) copy-start(bf16[2048,1024]{1,0:T(8,128)(2,1)} %all-gather.2.cloned.1.call-done.stats_ref) | copy-start | bytes 12582916
  98.5 1.4 %copy-start.1 = (bf16[1024,1024]{1,0:T(8,128)(2,1)}, bf16[1024,1024]{1,0:T(8,128)(2,1)S(1)}, u32[]{:S(2)}) copy-start(bf16[1024,1024]{1,0:T(8,128)(2,1)S(1)} %right_root.1.right_ref) | copy-start | bytes 6291460
  99.9 15.1 %copy-start.2 = (bf16[1024,1024]{1,0:T(8,128)(2,1)S(1)}, bf16[1024,1024]{1,0:T(8,128)(2,1)}, u32[]{:S(2)}) copy-start(bf16[1024,1024]{1,0:T(8,128)(2,1)} %copy-done.1) | copy-start | bytes 6291460
  115.5 1.3 collective-permute-start.16
  116.8 3.7 %collective-permute-start.17 = (f32[16,128]{1,0:T(8,128)S(1)}, f32[16,128]{1,0:T(8,128)S(1)}, u32[]{:S(2)}, u32[]{:S(2)}) collective-permute-start(f32[16,128]{1,0:T(8,128)S(1)} %add.9), channel_id=1, source_target_pairs={{0,2},{2,0},{4,6},{6,4},{1,3},{3,1},{5,7},{7,5},{8,10},{10,8},{12,... | collective-permute-start | bytes 24584 | tf_op jit(solution)/shard_map/ppermute | solution.py:25
  120.4 4.5 %collective-permute-start.18 = (f32[16,128]{1,0:T(8,128)S(1)}, f32[16,128]{1,0:T(8,128)S(1)}, u32[]{:S(2)}, u32[]{:S(2)}) collective-permute-start(f32[16,128]{1,0:T(8,128)S(1)} %add.10), channel_id=1, source_target_pairs={{0,4},{2,6},{4,0},{6,2},{1,5},{3,7},{5,1},{7,3},{8,12},{10,14},{12... | collective-permute-start | bytes 24584 | tf_op jit(solution)/shard_map/ppermute | solution.py:25
Sparse Core Ops, SparseCore 0:
  12.7 57.6 all-gather.1

commit v2 on v1

--- a/solution.py
+++ b/solution.py
@@ -68,13 +68,13 @@
             last_down_ref[block, at] = narrow(mid_ref[count + block, at], down_ref[block, at])
 
 
-def ring_second(mid, up, down, axis):
+def pass_on(mid, up, down):
     count = mid.shape[0] // 2
     last = jax.ShapeDtypeStruct((count,) + mid.shape[1:], mid.dtype)
     last_up, last_down = call(
         pass_kernel, "pass_on", (last, last), [VMEM] * 3, (mid, up, down), flops=mid.size, moved=6 * mid.size
     )
-    return shift(last_up, axis, 1), shift(last_down, axis, -1)
+    return last_up, last_down
 
 
 def turn_kernel(place_ref, own_ref, up_ref, down_ref, last_up_ref, last_down_ref, next_up, next_down, next_mid, next_own, sum_ref):
@@ -137,10 +137,19 @@
     )
 
 
+CUT = 2
+
+
 def begin_blocks(grads_ref, moves, sems):
+    rows = grads_ref.shape[3] // CUT
     copies = [
-        pltpu.make_async_copy(grads_ref.at[where], out.at[slot], sems.at[i])
+        pltpu.make_async_copy(
+            grads_ref.at[where + (pl.ds(part * rows, rows),)],
+            out.at[slot, pl.ds(part * rows, rows)],
+            sems.at[CUT * i + part],
+        )
         for i, (where, out, slot) in enumerate(moves)
+        for part in range(CUT)
     ]
     for each in copies:
         each.start()
@@ -151,8 +160,29 @@
     return tuple(lax.rem(place_ref[which] + step, 4) for step in range(4))
 
 
-def send_kernel(place_ref, grads_ref, stats_ref, x_up, x_down, y_up, y_down, narrow_ref, sems, wide_ref):
+def trim(index, stats_ref, out_ref):
+    rows = stats_ref.shape[0]
+    half = rows // 2
+
+    def block(at):
+        return pl.ds(at % 4 * rows, rows)
+
+    out_ref[:, block(0)] = stats_ref[:, block(index)].astype(jnp.bfloat16)
+    out_ref[:, block(1)] = stats_ref[:, block(index + 1)].astype(jnp.bfloat16)
+    if index < 2:
+        opposite = stats_ref[:, pl.ds((index + 2) * rows, half)]
+    else:
+        opposite = stats_ref[pl.ds(half, half), block(index + 2)].T
+    out_ref[:, pl.ds(2 * rows, half)] = opposite.astype(jnp.bfloat16)
+
+
+def send_kernel(place_ref, grads_ref, stats_ref, x_up, x_down, y_up, y_down, own_ref, wide_ref, trim_ref, sems, more):
     x, y = steps(place_ref, 0), steps(place_ref, 1)
+    rows = wide_ref.shape[0] // 8
+    parts = [pl.ds(part * rows, rows) for part in range(8)]
+    stats_in = [pltpu.make_async_copy(stats_ref.at[at], wide_ref.at[at], more.at[i]) for i, at in enumerate(parts)]
+    for each in stats_in:
+        each.start()
     moves = []
     for i in range(2):
         moves += [
@@ -165,15 +195,37 @@
             ((1, y[2], 2 + i), y_down, i),
             ((1, y[3], i), y_down, 2 + i),
         ]
-    stats_copy = pltpu.make_async_copy(stats_ref, wide_ref, sems.at[16])
-    stats_copy.start()
     copies = begin_blocks(grads_ref, moves, sems)
-    stats_copy.wait()
-    for row in range(0, wide_ref.shape[0], 32):
-        at = pl.ds(row, 32)
-        narrow_ref[at] = wide_ref[at].astype(jnp.bfloat16)
-    for each in copies:
+    for each in stats_in:
         each.wait()
+    for index in range(4):
+        pl.when(place_ref[2] == index)(functools.partial(trim, index, wide_ref, trim_ref))
+    stats_out = [pltpu.make_async_copy(trim_ref.at[at], own_ref.at[at], more.at[8 + i]) for i, at in enumerate(parts)]
+    for each in stats_out:
+        each.start()
+    for each in copies + stats_out:
+        each.wait()
+
+
+def send(place, grads, stats):
+    payload = jax.ShapeDtypeStruct((4,) + grads.shape[3:], grads.dtype)
+    rows = stats.shape[0]
+    own = jax.ShapeDtypeStruct((rows, 2 * rows + rows // 2), jnp.bfloat16)
+    return pl.pallas_call(
+        send_kernel,
+        out_shape=(payload,) * 4 + (own,),
+        in_specs=[SMEM, HBM, HBM],
+        out_specs=(VMEM,) * 4 + (HBM,),
+        scratch_shapes=[
+            pltpu.VMEM(stats.shape, stats.dtype),
+            pltpu.VMEM(own.shape, own.dtype),
+            pltpu.SemaphoreType.DMA((16 * CUT,)),
+            pltpu.SemaphoreType.DMA((16,)),
+        ],
+        compiler_params=pltpu.CompilerParams(vmem_limit_bytes=48 * 2**20),
+        cost_estimate=pl.CostEstimate(flops=0, bytes_accessed=2**23, transcendentals=0),
+        name="send",
+    )(place, grads, stats)
 
 
 def keep_kernel(place_ref, grads_ref, x_mid, x_own, y_mid, y_own, sems):
@@ -192,67 +244,107 @@
         each.wait()
 
 
-def pack(kernel, place, grads, stats=None):
-    mib = 16 if stats is None else 48
-    outs = (jax.ShapeDtypeStruct((4,) + grads.shape[3:], grads.dtype),) * 4
-    specs, operands = [SMEM, HBM], (place, grads)
-    scratch = [pltpu.SemaphoreType.DMA((17,))]
-    if stats is not None:
-        outs += (jax.ShapeDtypeStruct(stats.shape, jnp.bfloat16),)
-        specs, operands = specs + [HBM], operands + (stats,)
-        scratch += [pltpu.VMEM(stats.shape, stats.dtype)]
-    return call(kernel, kernel.__name__[:4], outs, specs, operands, scratch=scratch, mib=mib, moved=2**23)
-
-
-def root_kernel(side, offset_ref, stats_ref, out_ref, start_ref, first_ref, second_ref, third_ref):
+def keep(place, grads):
+    payload = jax.ShapeDtypeStruct((4,) + grads.shape[3:], grads.dtype)
+    return call(
+        keep_kernel,
+        "keep",
+        (payload,) * 4,
+        [SMEM, HBM],
+        (place, grads),
+        scratch=[pltpu.SemaphoreType.DMA((16 * CUT,))],
+        moved=2**23,
+    )
+
+
+def half_kernel(side, offset_ref, stats_ref, first_ref, second_ref, start_ref):
+    size = first_ref.shape[0]
+    slot = size // 4
+    half = slot // 2
+
+    def span(tile):
+        return pl.ds(tile * slot, slot)
+
+    def held(tile, columns):
+        position = lax.rem(offset_ref[0] + (4 * side + tile), 8)
+        return stats_ref[pl.ds(pl.multiple_of(position * slot, slot), slot), columns].astype(jnp.float32)
+
+    diagonal, following, opposite = pl.ds(0, slot), pl.ds(slot, slot), pl.ds(2 * slot, half)
+    total = jnp.zeros((8, slot // 2), jnp.float32)
+    for tile in range(4):
+        for columns, weight in ((diagonal, 1.0), (following, 2.0), (opposite, 2.0)):
+            values = held(tile, columns)
+            total = total + weight * lanes(values * values)
+    inverse = 1.0 / jnp.sqrt(jnp.sum(total))
+
+    row_ids = lax.broadcasted_iota(jnp.int32, (slot, slot), 0)
+    col_ids = lax.broadcasted_iota(jnp.int32, (slot, slot), 1)
+    eye = jnp.where(row_ids == col_ids, 1.0, 0.0).astype(jnp.float32)
+
+    def place(row, column, normed, on_diagonal):
+        start_ref[span(row), span(column)] = normed.astype(jnp.bfloat16)
+        term = 1.5 * eye - 0.5 * normed if on_diagonal else -0.5 * normed
+        first_ref[span(row), span(column)] = term.astype(jnp.bfloat16)
+
+    for tile in range(4):
+        after = (tile + 1) % 4
+        place(tile, tile, held(tile, diagonal) * inverse, True)
+        normed = held(tile, following) * inverse
+        place(tile, after, normed, False)
+        place(after, tile, normed.T, False)
+    for tile in range(2):
+        parts = [held(at, opposite) * inverse for at in (tile, tile + 2)]
+        normed = jnp.concatenate(parts, axis=1)
+        place(tile, tile + 2, normed, False)
+        place(tile + 2, tile, normed.T, False)
+
+    for tile in range(4):
+        product = jnp.dot(start_ref[span(tile), :], first_ref[...], preferred_element_type=jnp.float32)
+        second_ref[span(tile), :] = product.astype(jnp.bfloat16)
+
+
+def root_kernel(first_ref, second_ref, out_ref, third_ref):
     size = out_ref.shape[0]
     slot = size // 4
-
-    def eye_rows(tile):
+    for tile in range(4):
+        at = pl.ds(tile * slot, slot)
         row_ids = lax.broadcasted_iota(jnp.int32, (slot, size), 0) + tile * slot
         col_ids = lax.broadcasted_iota(jnp.int32, (slot, size), 1)
-        return jnp.where(row_ids == col_ids, 1.0, 0.0).astype(jnp.float32)
-
-    def rows(tile):
-        return pl.ds(tile * slot, slot)
-
-    def held(tile):
-        at = lax.rem(offset_ref[0] + side * 4 + tile, 8)
-        return stats_ref[pl.ds(pl.multiple_of(at * slot, slot), slot), :].astype(jnp.float32)
-
-    total = jnp.zeros((1, size), jnp.float32)
+        eye = jnp.where(row_ids == col_ids, 1.0, 0.0).astype(jnp.float32)
+        product = jnp.dot(first_ref[at, :], second_ref[...], preferred_element_type=jnp.float32)
+        third_ref[at, :] = (1.5 * eye - 0.5 * product).astype(jnp.bfloat16)
     for tile in range(4):
-        values = held(tile)
-        total = total + jnp.sum(values * values, axis=0, keepdims=True)
-    inverse = 1.0 / jnp.sqrt(jnp.sum(total))
-
-    for tile in range(4):
-        normed = held(tile) * inverse
-        start_ref[rows(tile), :] = normed.astype(jnp.bfloat16)
-        first_ref[rows(tile), :] = (1.5 * eye_rows(tile) - 0.5 * normed).astype(jnp.bfloat16)
-    for tile in range(4):
-        product = jnp.dot(start_ref[rows(tile), :], first_ref[...], preferred_element_type=jnp.float32)
-        second_ref[rows(tile), :] = product.astype(jnp.bfloat16)
-    for tile in range(4):
-        product = jnp.dot(first_ref[rows(tile), :], second_ref[...], preferred_element_type=jnp.float32)
-        third_ref[rows(tile), :] = (1.5 * eye_rows(tile) - 0.5 * product).astype(jnp.bfloat16)
-    for tile in range(4):
-        product = jnp.dot(third_ref[rows(tile), :], first_ref[...], preferred_element_type=jnp.float32)
-        out_ref[rows(tile), :] = product.astype(jnp.bfloat16)
-
-
-def inverse_root(side, stats, offset):
-    size = stats.shape[1]
-    return call(
-        functools.partial(root_kernel, side),
-        ("left_root", "right_root")[side],
-        jax.ShapeDtypeStruct((size, size), jnp.bfloat16),
+        at = pl.ds(tile * slot, slot)
+        product = jnp.dot(third_ref[at, :], first_ref[...], preferred_element_type=jnp.float32)
+        out_ref[at, :] = product.astype(jnp.bfloat16)
+
+
+def half_root(side, offset, stats):
+    size = stats.shape[0] // 2
+    matrix = jax.ShapeDtypeStruct((size, size), jnp.bfloat16)
+    return call(
+        functools.partial(half_kernel, side),
+        ("left_half", "right_half")[side],
+        (matrix, matrix),
         [SMEM, VMEM],
         (offset, stats),
-        scratch=[pltpu.VMEM((size, size), jnp.bfloat16)] * 4,
-        mib=24,
-        flops=6 * size**3,
+        scratch=[pltpu.VMEM((size, size), jnp.bfloat16)],
+        flops=2 * size**3,
         moved=4 * size * size,
+    )
+
+
+def inverse_root(first, second):
+    size = first.shape[0]
+    return call(
+        root_kernel,
+        "root",
+        jax.ShapeDtypeStruct((size, size), jnp.bfloat16),
+        [VMEM] * 2,
+        (first, second),
+        scratch=[pltpu.VMEM((size, size), jnp.bfloat16)],
+        flops=4 * size**3,
+        moved=6 * size * size,
     )
 
 
@@ -342,42 +434,47 @@
     )
 
 
+def after(dep, *values):
+    return lax.optimization_barrier((dep,) + values)[1:]
+
+
 def local(grad_partial, factor_stats, owner_table):
     size = grad_partial.shape[3]
     rows_here = grad_partial.shape[2]
     owner = ("zl", "c")
     grads = grad_partial.reshape(2, 4, 4, rows_here, size)
-    x, y = lax.axis_index("x").astype(jnp.int32), lax.axis_index("y").astype(jnp.int32)
-    place = jnp.stack((x, y))
-
-    x_up, x_down, y_up, y_down, own = pack(send_kernel, place, grads, factor_stats[0, 0])
-    place, x_up, own = lax.optimization_barrier((place, x_up, own))
+    zh, y, x, zl, c = (lax.axis_index(axis).astype(jnp.int32) for axis in FINE)
+    slot = (2 * zl + c - owner_table[0] + 8) % 4
+    place = jnp.stack((x, y, slot))
+
+    x_up, x_down, y_up, y_down, own = send(place, grads, factor_stats[0, 0])
     stats = lax.all_gather(own, owner, axis=0, tiled=True)
     x_ends = ring_first(x_up, x_down, "x")
     y_ends = ring_first(y_up, y_down, "y")
-    x_mid, x_own, y_mid, y_own = pack(keep_kernel, place, grads)
-
-    x_last = ring_second(x_mid, *x_ends, "x")
-    y_last = ring_second(y_mid, *y_ends, "y")
+    x_mid, x_own, y_mid, y_own = keep(*after(x_up, place), grads)
+
+    x_last = ring_first(*pass_on(x_mid, *x_ends), "x")
+    y_last = ring_first(*pass_on(y_mid, *y_ends), "y")
     lower_up, lower_down, lower_mid, lower_own = turn(y[None], x_own, *x_ends, *x_last)
     lower_ends = ring_first(lower_up, lower_down, "y")
     upper_up, upper_down, upper_mid, upper_own = turn(x[None], y_own, *y_ends, *y_last)
     upper_ends = ring_first(upper_up, upper_down, "x")
-    lower_last = ring_second(lower_mid, *lower_ends, "y")
-    upper_last = ring_second(upper_mid, *upper_ends, "x")
+    lower_last = ring_first(*pass_on(lower_mid, *lower_ends), "y")
+    upper_last = ring_first(*pass_on(upper_mid, *upper_ends), "x")
     pieces = make_pieces(lower_own, *lower_ends, *lower_last, upper_own, *upper_ends, *upper_last)
-    pieces, stats = lax.optimization_barrier((pieces, stats))
+
+    (stats,) = after(pieces, stats)
     pieces = lax.all_to_all(pieces, ("zh",) + owner, split_axis=0, concat_axis=0, tiled=True)
-    left_root = inverse_root(0, stats, owner_table)
-    right_root = inverse_root(1, stats, owner_table)
-
+    left_root = inverse_root(*half_root(0, owner_table, stats))
+    first, second = half_root(1, owner_table, stats)
+    (pieces,) = after(second, pieces)
     mixed, energy = mix(pieces, left_root)
-    mixed, right_root = lax.optimization_barrier((mixed, right_root))
+    (second,) = after(mixed, second)
     mixed = lax.all_to_all(mixed, owner, split_axis=0, concat_axis=0, tiled=True)
+    right_root = inverse_root(first, second)
     precond, totals = condition(mixed, right_root, energy)
     totals = totals + swap(totals, "c", 1)
-    totals = totals + swap(totals, "zl", 1)
-    totals = totals + swap(totals, "zl", 2)
+    totals = totals + shift(totals, "zl", 1) + shift(totals, "zl", 2) + shift(totals, "zl", 3)
     return finish(totals, precond, float(size * size))[None]
 
 

time: 134 us -> 137 us (1.022)
  blocking collectives: 14.3 us -> 0 us
  starting transfers between devices: 31.2 us -> 38.5 us
  Pallas kernels: 24.6 us -> 31.7 us
  local copies, waits for them, and re-layouts: 9.15 us -> 16.1 us
  waiting for transfers between devices: 39.3 us -> 34.9 us
    all_to_all x1 -> x0, blocking collectives: 14.3 us -> none  [local(): lax.all_to_all(mixed, owner, split_axis=0, concat_axis=0, tiled=True)]
    ppermute x3 -> x1, waiting for transfers between devices: 9.19 us -> 1.16 us  [swap(): return lax.ppermute(array, axis, [(i, i ^ mask) for i in range(size)])]
    unnamed x12 -> x20, local copies, waits for them, and re-layouts: 9.15 us -> 16.1 us
    pallas_call x0 -> x1, Pallas kernels: none -> 4.68 us  [send(): pl.pallas_call(send_kernel, out_shape=(payload,) * 4 + (own,), in_specs=[...]
    all_to_all x0 -> x1, starting transfers between devices: none -> 3.98 us  [local(): lax.all_to_all(mixed, owner, split_axis=0, concat_axis=0, tiled=True)]
    all_to_all x1, waiting for transfers between devices: 0.01 us -> 3.96 us  [local(): lax.all_to_all(pieces, ('zh',) + owner, split_axis=0, concat_axis=0, tile...]
    ppermute x16 -> x19, starting transfers between devices: 22 us -> 25.9 us  [shift(): lax.ppermute(array, axis, [(i, (i + step) % size) for i in range(size)])]
    pallas_call x14 -> x15, Pallas kernels: 24.6 us -> 27 us  [call(): pl.pallas_call(kernel, out_shape=out_shape, in_specs=in_specs, out_specs=...]
  transfers between devices with their start and end apart: 21 -> 23, of which waited for: 10 -> 13; matrix products, arithmetic and copies ran while one was open for 0% -> 0% of each run, Pallas kernels for 14% -> 14%
where the time goes in v2:
time: 137 us; the launch traced here: 136 us
  starting transfers between devices  38.5 us (28%)
  waiting for transfers between devices  34.9 us (25%)
  Pallas kernels  31.7 us (23%)
  local copies, waits for them, and re-layouts  16.1 us (12%)
  between operations  14.3 us (10%)
    ppermute x19, waiting for transfers between devices, shift(): lax.ppermute(array, axis, [(i, (i + step) % size) for i in range(size)])  27.7 us
    pallas_call x15, Pallas kernels, call(): pl.pallas_call(kernel, out_shape=out_shape, in_specs=in_specs, out_specs=...  27 us
    ppermute x19, starting transfers between devices, shift(): lax.ppermute(array, axis, [(i, (i + step) % size) for i in range(size)])  25.9 us
    unnamed x20, local copies, waits for them, and re-layouts  16.1 us
    all_to_all x1, starting transfers between devices, local(): lax.all_to_all(pieces, ('zh',) + owner, split_axis=0, concat_axis=0, tile...  8.58 us
    pallas_call x1, Pallas kernels, send(): pl.pallas_call(send_kernel, out_shape=(payload,) * 4 + (own,), in_specs=[...  4.68 us
    all_to_all x1, starting transfers between devices, local(): lax.all_to_all(mixed, owner, split_axis=0, concat_axis=0, tiled=True)  3.98 us
    all_to_all x1, waiting for transfers between devices, local(): lax.all_to_all(pieces, ('zh',) + owner, split_axis=0, concat_axis=0, tile...  3.96 us
  transfers between devices with their start and end apart: 23, of which 13 were waited for; matrix products, arithmetic and copies ran while one was open for 0% of the time, Pallas kernels for 14%

profile of v2, /device:TPU:6, one launch (start us, length us, event | category | flops | bytes accessed | tf_op | source)
XLA Modules:
  0.0 135.6 jit_solution(8018709500874471530)
XLA Ops:
  8.5 4.7 %send.1 = (bf16[4,128,1024]{2,1,0:T(8,128)(2,1)S(1)}, bf16[4,128,1024]{2,1,0:T(8,128)(2,1)S(1)}, bf16[4,128,1024]{2,1,0:T(8,128)(2,1)S(1)}, bf16[4,128,1024]{2,1,0:T(8,128)(2,1)S(1)}, bf16[256,640]{1,0:T(8,128)(2,1)}) custom-call(s32[3]{0:T(128)S(1)} %pad_add_fusion.place_ref, bf16[2,4,4,128,1024]{4,3,2,1,0:T(8,128)(2,1)} %bitcast.8, f32[256,1024]{1,0:T(8,128)S(1)} %bitcast.10), custom_call_target="tpu_custom_call" | custom-call | bytes 8388608 | tf_op jit(solution)/shard_map/send/pallas_call | solution.py:214
  14.2 1.7 %collective-permute-start.8 = (bf16[4,128,1024]{2,1,0:T(8,128)(2,1)}, bf16[4,128,1024]{2,1,0:T(8,128)(2,1)S(1)}, u32[]{:S(2)}, u32[]{:S(2)}) collective-permute-start(bf16[4,128,1024]{2,1,0:T(8,128)(2,1)} %copy-done.3), channel_id=1, source_target_pairs={{0,32},{32,64},{64,96},{96,0},{1,33},{33,65},{65,97},{97,1},{2,34}... | collective-permute-start | bytes 3145736 | tf_op jit(solution)/shard_map/ppermute | solution.py:20
  15.9 1.7 %collective-permute-start.9 = (bf16[4,128,1024]{2,1,0:T(8,128)(2,1)S(1)}, bf16[4,128,1024]{2,1,0:T(8,128)(2,1)S(1)}, u32[]{:S(2)}, u32[]{:S(2)}) collective-permute-start(bf16[4,128,1024]{2,1,0:T(8,128)(2,1)S(1)} %get-tuple-element.57), channel_id=1, source_target_pairs={{0,96},{32,0},{64,32},{96,64},{1,97},{33,1},{65,33},{97,65},{2,98}... | collective-permute-start | bytes 3145736 | tf_op jit(solution)/shard_map/ppermute | solution.py:20
  17.6 2.2 %collective-permute-start = (bf16[4,128,1024]{2,1,0:T(8,128)(2,1)S(1)}, bf16[4,128,1024]{2,1,0:T(8,128)(2,1)S(1)}, u32[]{:S(2)}, u32[]{:S(2)}) collective-permute-start(bf16[4,128,1024]{2,1,0:T(8,128)(2,1)S(1)} %get-tuple-element.42), channel_id=1, source_target_pairs={{0,8},{8,16},{16,24},{24,0},{1,9},{9,17},{17,25},{25,1},{2,10},{10... | collective-permute-start | bytes 3145736 | tf_op jit(solution)/shard_map/ppermute | solution.py:20
  19.8 3.4 %copy-done = bf16[1,32,128,1024]{3,2,1,0:T(8,128)(2,1)S(1)} copy-done((bf16[1,32,128,1024]{3,2,1,0:T(8,128)(2,1)S(1)}, bf16[1,32,128,1024]{3,2,1,0:T(8,128)(2,1)}, u32[]{:S(2)}) %copy-start) | copy-done | bytes 8388632
  23.2 6.3 %keep.1 = (bf16[4,128,1024]{2,1,0:T(8,128)(2,1)S(1)}, bf16[4,128,1024]{2,1,0:T(8,128)(2,1)S(1)}, bf16[4,128,1024]{2,1,0:T(8,128)(2,1)S(1)}, bf16[4,128,1024]{2,1,0:T(8,128)(2,1)S(1)}) custom-call(s32[3]{0:T(128)S(1)} %pad_add_fusion.place_ref, bf16[2,4,4,128,1024]{4,3,2,1,0:T(8,128)(2,1)S(1)} %bitcast.9), custom_call_target="tpu_custom_call" | custom-call | bytes 8388608 | tf_op jit(solution)/shard_map/keep/pallas_call | solution.py:46
  29.5 11.2 %collective-permute-done.8.up_ref = bf16[4,128,1024]{2,1,0:T(8,128)(2,1)S(1)} collective-permute-done((bf16[4,128,1024]{2,1,0:T(8,128)(2,1)}, bf16[4,128,1024]{2,1,0:T(8,128)(2,1)S(1)}, u32[]{:S(2)}, u32[]{:S(2)}) %collective-permute-start.8) | collective-permute-done | bytes 1048608 | tf_op jit(solution)/shard_map/ppermute | solution.py:20
  41.0 1.5 %collective-permute-start.10 = (bf16[2,128,1024]{2,1,0:T(8,128)(2,1)S(1)}, bf16[2,128,1024]{2,1,0:T(8,128)(2,1)S(1)}, u32[]{:S(2)}, u32[]{:S(2)}) collective-permute-start(bf16[2,128,1024]{2,1,0:T(8,128)(2,1)S(1)} %get-tuple-element.59), channel_id=1, source_target_pairs={{0,32},{32,64},{64,96},{96,0},{1,33},{33,65},{65,97},{97,1},{2,34}... | collective-permute-start | bytes 1572872 | tf_op jit(solution)/shard_map/ppermute | solution.py:20
  42.4 1.9 %collective-permute-start.11 = (bf16[2,128,1024]{2,1,0:T(8,128)(2,1)S(1)}, bf16[2,128,1024]{2,1,0:T(8,128)(2,1)S(1)}, u32[]{:S(2)}, u32[]{:S(2)}) collective-permute-start(bf16[2,128,1024]{2,1,0:T(8,128)(2,1)S(1)} %get-tuple-element.60), channel_id=1, source_target_pairs={{0,96},{32,0},{64,32},{96,64},{1,97},{33,1},{65,33},{97,65},{2,98}... | collective-permute-start | bytes 1572872 | tf_op jit(solution)/shard_map/ppermute | solution.py:20
  45.1 1.5 %collective-permute-start.3 = (bf16[2,128,1024]{2,1,0:T(8,128)(2,1)S(1)}, bf16[2,128,1024]{2,1,0:T(8,128)(2,1)S(1)}, u32[]{:S(2)}, u32[]{:S(2)}) collective-permute-start(bf16[2,128,1024]{2,1,0:T(8,128)(2,1)S(1)} %get-tuple-element.48), channel_id=1, source_target_pairs={{0,24},{8,0},{16,8},{24,16},{1,25},{9,1},{17,9},{25,17},{2,26},{10... | collective-permute-start | bytes 1572872 | tf_op jit(solution)/shard_map/ppermute | solution.py:20
  46.6 8.6 %collective-permute-done.10.last_up_ref = bf16[2,128,1024]{2,1,0:T(8,128)(2,1)S(1)} collective-permute-done((bf16[2,128,1024]{2,1,0:T(8,128)(2,1)S(1)}, bf16[2,128,1024]{2,1,0:T(8,128)(2,1)S(1)}, u32[]{:S(2)}, u32[]{:S(2)}) %collective-permute-start.10) | collective-permute-done | bytes 524320 | tf_op jit(solution)/shard_map/ppermute | solution.py:20
  55.8 2.0 %collective-permute-start.13 = (bf16[2,64,1024]{2,1,0:T(8,128)(2,1)S(1)}, bf16[2,64,1024]{2,1,0:T(8,128)(2,1)S(1)}, u32[]{:S(2)}, u32[]{:S(2)}) collective-permute-start(bf16[2,64,1024]{2,1,0:T(8,128)(2,1)S(1)} %get-tuple-element.63), channel_id=1, source_target_pairs={{0,24},{8,0},{16,8},{24,16},{1,25},{9,1},{17,9},{25,17},{2,26},{10... | collective-permute-start | bytes 786440 | tf_op jit(solution)/shard_map/ppermute | solution.py:20
  59.1 3.2 %collective-permute-start.5 = (bf16[2,64,1024]{2,1,0:T(8,128)(2,1)S(1)}, bf16[2,64,1024]{2,1,0:T(8,128)(2,1)S(1)}, u32[]{:S(2)}, u32[]{:S(2)}) collective-permute-start(bf16[2,64,1024]{2,1,0:T(8,128)(2,1)S(1)} %get-tuple-element.51), channel_id=1, source_target_pairs={{0,96},{32,0},{64,32},{96,64},{1,97},{33,1},{65,33},{97,65},{2,98}... | collective-permute-start | bytes 786440 | tf_op jit(solution)/shard_map/ppermute | solution.py:20
  64.6 1.6 %collective-permute-start.15 = (bf16[1,64,1024]{2,1,0:T(8,128)(2,1)S(1)}, bf16[1,64,1024]{2,1,0:T(8,128)(2,1)S(1)}, u32[]{:S(2)}, u32[]{:S(2)}) collective-permute-start(bf16[1,64,1024]{2,1,0:T(8,128)(2,1)S(1)} %get-tuple-element.66), channel_id=1, source_target_pairs={{0,24},{8,0},{16,8},{24,16},{1,25},{9,1},{17,9},{25,17},{2,26},{10... | collective-permute-start | bytes 393224 | tf_op jit(solution)/shard_map/ppermute | solution.py:20
  67.4 2.8 %collective-permute-start.7 = (bf16[1,64,1024]{2,1,0:T(8,128)(2,1)S(1)}, bf16[1,64,1024]{2,1,0:T(8,128)(2,1)S(1)}, u32[]{:S(2)}, u32[]{:S(2)}) collective-permute-start(bf16[1,64,1024]{2,1,0:T(8,128)(2,1)S(1)} %get-tuple-element.54), channel_id=1, source_target_pairs={{0,96},{32,0},{64,32},{96,64},{1,97},{33,1},{65,33},{97,65},{2,98}... | collective-permute-start | bytes 393224 | tf_op jit(solution)/shard_map/ppermute | solution.py:20
  70.8 2.2 %collective-permute-done.6.refs_3_ = bf16[1,64,1024]{2,1,0:T(8,128)(2,1)S(1)} collective-permute-done((bf16[1,64,1024]{2,1,0:T(8,128)(2,1)S(1)}, bf16[1,64,1024]{2,1,0:T(8,128)(2,1)S(1)}, u32[]{:S(2)}, u32[]{:S(2)}) %collective-permute-start.6) | collective-permute-done | bytes 131104 | tf_op jit(solution)/shard_map/ppermute | solution.py:20
  74.0 8.6 %all-to-all-start = ((bf16[16,128,128]{2,1,0:T(8,128)(2,1)}), bf16[16,128,128]{2,1,0:T(8,128)(2,1)S(1)}, u32[]{:S(2)}, u32[]{:S(2)}) async-start(bf16[16,128,128]{2,1,0:T(8,128)(2,1)} %pieces.1), calls=%async_computation | async-start | bytes 1048576 | tf_op jit(solution)/shard_map/all_to_all | solution.py:467
  82.6 1.7 %copy-done.2 = bf16[2048,640]{1,0:T(8,128)(2,1)S(1)} copy-done((bf16[2048,640]{1,0:T(8,128)(2,1)S(1)}, bf16[2048,640]{1,0:T(8,128)(2,1)}, u32[]{:S(2)}) %copy-start.2) | copy-done | bytes 2621464
  84.4 3.1 %left_half.1 = (bf16[1024,1024]{1,0:T(8,128)(2,1)S(1)}, bf16[1024,1024]{1,0:T(8,128)(2,1)S(1)}) custom-call(s32[1]{0:T(128)} %copy.4.offset_ref, bf16[2048,640]{1,0:T(8,128)(2,1)S(1)} %copy-done.2), custom_call_target="tpu_custom_call" | custom-call | flops 2147483648 | bytes 4194304 | tf_op jit(solution)/shard_map/left_half/pallas_call | solution.py:46
  88.8 3.1 %right_half.1 = (bf16[1024,1024]{1,0:T(8,128)(2,1)S(1)}, bf16[1024,1024]{1,0:T(8,128)(2,1)S(1)}) custom-call(s32[1]{0:T(128)} %copy.4.offset_ref, bf16[2048,640]{1,0:T(8,128)(2,1)S(1)} %copy-done.2), custom_call_target="tpu_custom_call" | custom-call | flops 2147483648 | bytes 4194304 | tf_op jit(solution)/shard_map/right_half/pallas_call | solution.py:46
  94.7 4.0 %all-to-all-done.pieces_ref = bf16[16,128,128]{2,1,0:T(8,128)(2,1)S(1)} async-done(((bf16[16,128,128]{2,1,0:T(8,128)(2,1)}), bf16[16,128,128]{2,1,0:T(8,128)(2,1)S(1)}, u32[]{:S(2)}, u32[]{:S(2)}) %all-to-all-start) | async-done | bytes 524320 | tf_op jit(solution)/shard_map/all_to_all | solution.py:467
  98.6 1.6 %copy-done.9 = bf16[1024,1024]{1,0:T(8,128)(2,1)S(1)} copy-done((bf16[1024,1024]{1,0:T(8,128)(2,1)S(1)}, bf16[1024,1024]{1,0:T(8,128)(2,1)}, u32[]{:S(2)}) %copy-start.9) | copy-done | bytes 2097176
  100.2 4.5 %root.2.left_ref = bf16[1024,1024]{1,0:T(8,128)(2,1)S(1)} custom-call(bf16[1024,1024]{1,0:T(8,128)(2,1)S(1)} %get-tuple-element.71.first_ref, bf16[1024,1024]{1,0:T(8,128)(2,1)S(1)} %copy-done.9), custom_call_target="tpu_custom_call" | custom-call | flops 4294967296 | bytes 6291456 | tf_op jit(solution)/shard_map/root/pallas_call | solution.py:46
  104.7 1.5 %mix.1 = (bf16[8,128,128]{2,1,0:T(8,128)(2,1)}, f32[8,128]{1,0:T(8,128)S(1)}) custom-call(bf16[16,128,128]{2,1,0:T(8,128)(2,1)S(1)} %all-to-all-done.pieces_ref, bf16[1024,1024]{1,0:T(8,128)(2,1)S(1)} %root.2.left_ref), custom_call_target="tpu_custom_call" | custom-call | flops 268435456 | bytes 2097152 | tf_op jit(solution)/shard_map/mix/pallas_call | solution.py:46
  106.2 4.0 %all-to-all-start.1 = ((bf16[8,128,128]{2,1,0:T(8,128)(2,1)}), bf16[8,128,128]{2,1,0:T(8,128)(2,1)S(1)}, u32[]{:S(2)}, u32[]{:S(2)}) async-start(bf16[8,128,128]{2,1,0:T(8,128)(2,1)} %get-tuple-element.73), calls=%async_computation.1 | async-start | bytes 524288 | tf_op jit(solution)/shard_map/all_to_all | solution.py:473
  110.2 1.6 %copy-done.5 = bf16[1024,1024]{1,0:T(8,128)(2,1)S(1)} copy-done((bf16[1024,1024]{1,0:T(8,128)(2,1)S(1)}, bf16[1024,1024]{1,0:T(8,128)(2,1)}, u32[]{:S(2)}) %copy-start.5) | copy-done | bytes 2097176
  111.8 1.6 %copy-done.7 = bf16[1024,1024]{1,0:T(8,128)(2,1)S(1)} copy-done((bf16[1024,1024]{1,0:T(8,128)(2,1)S(1)}, bf16[1024,1024]{1,0:T(8,128)(2,1)}, u32[]{:S(2)}) %copy-start.7) | copy-done | bytes 2097176
  113.4 4.5 %root.3.right_ref = bf16[1024,1024]{1,0:T(8,128)(2,1)S(1)} custom-call(bf16[1024,1024]{1,0:T(8,128)(2,1)S(1)} %copy-done.5, bf16[1024,1024]{1,0:T(8,128)(2,1)S(1)} %copy-done.7), custom_call_target="tpu_custom_call" | custom-call | flops 4294967296 | bytes 6291456 | tf_op jit(solution)/shard_map/root/pallas_call | solution.py:46
  117.9 2.0 %all-to-all-done.1.mixed_ref = bf16[8,128,128]{2,1,0:T(8,128)(2,1)S(1)} async-done(((bf16[8,128,128]{2,1,0:T(8,128)(2,1)}), bf16[8,128,128]{2,1,0:T(8,128)(2,1)S(1)}, u32[]{:S(2)}, u32[]{:S(2)}) %all-to-all-start.1) | async-done | bytes 262176 | tf_op jit(solution)/shard_map/all_to_all | solution.py:473
  121.9 2.2 %collective-permute-start.18 = (f32[16,128]{1,0:T(8,128)S(1)}, f32[16,128]{1,0:T(8,128)S(1)}, u32[]{:S(2)}, u32[]{:S(2)}) collective-permute-start(f32[16,128]{1,0:T(8,128)S(1)} %add.25), channel_id=1, source_target_pairs={{0,4},{2,6},{4,0},{6,2},{1,5},{3,7},{5,1},{7,3},{8,12},{10,14},{12... | collective-permute-start | bytes 24584 | tf_op jit(solution)/shard_map/ppermute | solution.py:20
  124.1 1.5 %collective-permute-start.19 = (f32[16,128]{1,0:T(8,128)S(1)}, f32[16,128]{1,0:T(8,128)S(1)}, u32[]{:S(2)}, u32[]{:S(2)}) collective-permute-start(f32[16,128]{1,0:T(8,128)S(1)} %add.25), channel_id=1, source_target_pairs={{0,6},{2,0},{4,2},{6,4},{1,7},{3,1},{5,3},{7,5},{8,14},{10,8},{12,... | collective-permute-start | bytes 24584 | tf_op jit(solution)/shard_map/ppermute | solution.py:20
  125.5 1.6 %collective-permute-done.17 = f32[16,128]{1,0:T(8,128)S(1)} collective-permute-done((f32[16,128]{1,0:T(8,128)S(1)}, f32[16,128]{1,0:T(8,128)S(1)}, u32[]{:S(2)}, u32[]{:S(2)}) %collective-permute-start.17) | collective-permute-done | bytes 8224 | tf_op jit(solution)/shard_map/ppermute | solution.py:20
  (54 shorter events, 17.8 us)
Async XLA Ops:
  6.5 76.1 %all-gather.2.cloned.1.call-start = ((), (), s32[]{:S(2)}) async-start(), calls=%async_computation.2 | async-start | bytes 2949120 | tf_op jit(solution)/shard_map/all_gather | solution.py:451
  7.3 1.2 copy-start.1
  14.2 26.5 %collective-permute-start.8 = (bf16[4,128,1024]{2,1,0:T(8,128)(2,1)}, bf16[4,128,1024]{2,1,0:T(8,128)(2,1)S(1)}, u32[]{:S(2)}, u32[]{:S(2)}) collective-permute-start(bf16[4,128,1024]{2,1,0:T(8,128)(2,1)} %copy-done.3), channel_id=1, source_target_pairs={{0,32},{32,64},{64,96},{96,0},{1,33},{33,65},{65,97},{97,1},{2,34}... | collective-permute-start | bytes 3145736 | tf_op jit(solution)/shard_map/ppermute | solution.py:20
  15.9 24.8 %collective-permute-start.9 = (bf16[4,128,1024]{2,1,0:T(8,128)(2,1)S(1)}, bf16[4,128,1024]{2,1,0:T(8,128)(2,1)S(1)}, u32[]{:S(2)}, u32[]{:S(2)}) collective-permute-start(bf16[4,128,1024]{2,1,0:T(8,128)(2,1)S(1)} %get-tuple-element.57), channel_id=1, source_target_pairs={{0,96},{32,0},{64,32},{96,64},{1,97},{33,1},{65,33},{97,65},{2,98}... | collective-permute-start | bytes 3145736 | tf_op jit(solution)/shard_map/ppermute | solution.py:20
  17.6 26.7 %collective-permute-start = (bf16[4,128,1024]{2,1,0:T(8,128)(2,1)S(1)}, bf16[4,128,1024]{2,1,0:T(8,128)(2,1)S(1)}, u32[]{:S(2)}, u32[]{:S(2)}) collective-permute-start(bf16[4,128,1024]{2,1,0:T(8,128)(2,1)S(1)} %get-tuple-element.42), channel_id=1, source_target_pairs={{0,8},{8,16},{16,24},{24,0},{1,9},{9,17},{17,25},{25,1},{2,10},{10... | collective-permute-start | bytes 3145736 | tf_op jit(solution)/shard_map/ppermute | solution.py:20
  19.8 24.5 %collective-permute-start.1 = (bf16[4,128,1024]{2,1,0:T(8,128)(2,1)S(1)}, bf16[4,128,1024]{2,1,0:T(8,128)(2,1)S(1)}, u32[]{:S(2)}, u32[]{:S(2)}) collective-permute-start(bf16[4,128,1024]{2,1,0:T(8,128)(2,1)S(1)} %get-tuple-element.45), channel_id=1, source_target_pairs={{0,24},{8,0},{16,8},{24,16},{1,25},{9,1},{17,9},{25,17},{2,26},{10... | collective-permute-start | bytes 3145736 | tf_op jit(solution)/shard_map/ppermute | solution.py:20
  19.8 3.4 %copy-start = (bf16[1,32,128,1024]{3,2,1,0:T(8,128)(2,1)S(1)}, bf16[1,32,128,1024]{3,2,1,0:T(8,128)(2,1)}, u32[]{:S(2)}) copy-start(bf16[1,32,128,1024]{3,2,1,0:T(8,128)(2,1)} %param.3) | copy-start | bytes 25165828
  41.0 14.3 %collective-permute-start.10 = (bf16[2,128,1024]{2,1,0:T(8,128)(2,1)S(1)}, bf16[2,128,1024]{2,1,0:T(8,128)(2,1)S(1)}, u32[]{:S(2)}, u32[]{:S(2)}) collective-permute-start(bf16[2,128,1024]{2,1,0:T(8,128)(2,1)S(1)} %get-tuple-element.59), channel_id=1, source_target_pairs={{0,32},{32,64},{64,96},{96,0},{1,33},{33,65},{65,97},{97,1},{2,34}... | collective-permute-start | bytes 1572872 | tf_op jit(solution)/shard_map/ppermute | solution.py:20
  42.4 12.8 %collective-permute-start.11 = (bf16[2,128,1024]{2,1,0:T(8,128)(2,1)S(1)}, bf16[2,128,1024]{2,1,0:T(8,128)(2,1)S(1)}, u32[]{:S(2)}, u32[]{:S(2)}) collective-permute-start(bf16[2,128,1024]{2,1,0:T(8,128)(2,1)S(1)} %get-tuple-element.60), channel_id=1, source_target_pairs={{0,96},{32,0},{64,32},{96,64},{1,97},{33,1},{65,33},{97,65},{2,98}... | collective-permute-start | bytes 1572872 | tf_op jit(solution)/shard_map/ppermute | solution.py:20
  44.5 13.3 %collective-permute-start.2 = (bf16[2,128,1024]{2,1,0:T(8,128)(2,1)S(1)}, bf16[2,128,1024]{2,1,0:T(8,128)(2,1)S(1)}, u32[]{:S(2)}, u32[]{:S(2)}) collective-permute-start(bf16[2,128,1024]{2,1,0:T(8,128)(2,1)S(1)} %get-tuple-element.47), channel_id=1, source_target_pairs={{0,8},{8,16},{16,24},{24,0},{1,9},{9,17},{17,25},{25,1},{2,10},{10... | collective-permute-start | bytes 1572872 | tf_op jit(solution)/shard_map/ppermute | solution.py:20
  45.1 13.5 %collective-permute-start.3 = (bf16[2,128,1024]{2,1,0:T(8,128)(2,1)S(1)}, bf16[2,128,1024]{2,1,0:T(8,128)(2,1)S(1)}, u32[]{:S(2)}, u32[]{:S(2)}) collective-permute-start(bf16[2,128,1024]{2,1,0:T(8,128)(2,1)S(1)} %get-tuple-element.48), channel_id=1, source_target_pairs={{0,24},{8,0},{16,8},{24,16},{1,25},{9,1},{17,9},{25,17},{2,26},{10... | collective-permute-start | bytes 1572872 | tf_op jit(solution)/shard_map/ppermute | solution.py:20
  55.7 6.9 %collective-permute-start.12 = (bf16[2,64,1024]{2,1,0:T(8,128)(2,1)S(1)}, bf16[2,64,1024]{2,1,0:T(8,128)(2,1)S(1)}, u32[]{:S(2)}, u32[]{:S(2)}) collective-permute-start(bf16[2,64,1024]{2,1,0:T(8,128)(2,1)S(1)} %get-tuple-element.62), channel_id=1, source_target_pairs={{0,8},{8,16},{16,24},{24,0},{1,9},{9,17},{17,25},{25,1},{2,10},{10... | collective-permute-start | bytes 786440 | tf_op jit(solution)/shard_map/ppermute | solution.py:20
  55.8 8.2 %collective-permute-start.13 = (bf16[2,64,1024]{2,1,0:T(8,128)(2,1)S(1)}, bf16[2,64,1024]{2,1,0:T(8,128)(2,1)S(1)}, u32[]{:S(2)}, u32[]{:S(2)}) collective-permute-start(bf16[2,64,1024]{2,1,0:T(8,128)(2,1)S(1)} %get-tuple-element.63), channel_id=1, source_target_pairs={{0,24},{8,0},{16,8},{24,16},{1,25},{9,1},{17,9},{25,17},{2,26},{10... | collective-permute-start | bytes 786440 | tf_op jit(solution)/shard_map/ppermute | solution.py:20
  59.0 7.7 %collective-permute-start.4 = (bf16[2,64,1024]{2,1,0:T(8,128)(2,1)S(1)}, bf16[2,64,1024]{2,1,0:T(8,128)(2,1)S(1)}, u32[]{:S(2)}, u32[]{:S(2)}) collective-permute-start(bf16[2,64,1024]{2,1,0:T(8,128)(2,1)S(1)} %get-tuple-element.50), channel_id=1, source_target_pairs={{0,32},{32,64},{64,96},{96,0},{1,33},{33,65},{65,97},{97,1},{2,34}... | collective-permute-start | bytes 786440 | tf_op jit(solution)/shard_map/ppermute | solution.py:20
  59.1 7.6 %collective-permute-start.5 = (bf16[2,64,1024]{2,1,0:T(8,128)(2,1)S(1)}, bf16[2,64,1024]{2,1,0:T(8,128)(2,1)S(1)}, u32[]{:S(2)}, u32[]{:S(2)}) collective-permute-start(bf16[2,64,1024]{2,1,0:T(8,128)(2,1)S(1)} %get-tuple-element.51), channel_id=1, source_target_pairs={{0,96},{32,0},{64,32},{96,64},{1,97},{33,1},{65,33},{97,65},{2,98}... | collective-permute-start | bytes 786440 | tf_op jit(solution)/shard_map/ppermute | solution.py:20
  64.0 6.2 %collective-permute-start.14 = (bf16[1,64,1024]{2,1,0:T(8,128)(2,1)S(1)}, bf16[1,64,1024]{2,1,0:T(8,128)(2,1)S(1)}, u32[]{:S(2)}, u32[]{:S(2)}) collective-permute-start(bf16[1,64,1024]{2,1,0:T(8,128)(2,1)S(1)} %get-tuple-element.65), channel_id=1, source_target_pairs={{0,8},{8,16},{16,24},{24,0},{1,9},{9,17},{17,25},{25,1},{2,10},{10... | collective-permute-start | bytes 393224 | tf_op jit(solution)/shard_map/ppermute | solution.py:20
  64.6 6.2 %collective-permute-start.15 = (bf16[1,64,1024]{2,1,0:T(8,128)(2,1)S(1)}, bf16[1,64,1024]{2,1,0:T(8,128)(2,1)S(1)}, u32[]{:S(2)}, u32[]{:S(2)}) collective-permute-start(bf16[1,64,1024]{2,1,0:T(8,128)(2,1)S(1)} %get-tuple-element.66), channel_id=1, source_target_pairs={{0,24},{8,0},{16,8},{24,16},{1,25},{9,1},{17,9},{25,17},{2,26},{10... | collective-permute-start | bytes 393224 | tf_op jit(solution)/shard_map/ppermute | solution.py:20
  66.8 6.3 %collective-permute-start.6 = (bf16[1,64,1024]{2,1,0:T(8,128)(2,1)S(1)}, bf16[1,64,1024]{2,1,0:T(8,128)(2,1)S(1)}, u32[]{:S(2)}, u32[]{:S(2)}) collective-permute-start(bf16[1,64,1024]{2,1,0:T(8,128)(2,1)S(1)} %get-tuple-element.53), channel_id=1, source_target_pairs={{0,32},{32,64},{64,96},{96,0},{1,33},{33,65},{65,97},{97,1},{2,34}... | collective-permute-start | bytes 393224 | tf_op jit(solution)/shard_map/ppermute | solution.py:20
  67.4 5.7 %collective-permute-start.7 = (bf16[1,64,1024]{2,1,0:T(8,128)(2,1)S(1)}, bf16[1,64,1024]{2,1,0:T(8,128)(2,1)S(1)}, u32[]{:S(2)}, u32[]{:S(2)}) collective-permute-start(bf16[1,64,1024]{2,1,0:T(8,128)(2,1)S(1)} %get-tuple-element.54), channel_id=1, source_target_pairs={{0,96},{32,0},{64,32},{96,64},{1,97},{33,1},{65,33},{97,65},{2,98}... | collective-permute-start | bytes 393224 | tf_op jit(solution)/shard_map/ppermute | solution.py:20
  74.0 24.6 %all-to-all-start = ((bf16[16,128,128]{2,1,0:T(8,128)(2,1)}), bf16[16,128,128]{2,1,0:T(8,128)(2,1)S(1)}, u32[]{:S(2)}, u32[]{:S(2)}) async-start(bf16[16,128,128]{2,1,0:T(8,128)(2,1)} %pieces.1), calls=%async_computation | async-start | bytes 1048576 | tf_op jit(solution)/shard_map/all_to_all | solution.py:467
  82.6 1.7 %copy-start.2 = (bf16[2048,640]{1,0:T(8,128)(2,1)S(1)}, bf16[2048,640]{1,0:T(8,128)(2,1)}, u32[]{:S(2)}) copy-start(bf16[2048,640]{1,0:T(8,128)(2,1)} %all-gather.2.cloned.1.call-done.stats_ref) | copy-start | bytes 7864324
  87.5 1.3 copy-start.8
  92.0 1.3 copy-start.4
  93.3 1.4 %copy-start.6 = (bf16[1024,1024]{1,0:T(8,128)(2,1)}, bf16[1024,1024]{1,0:T(8,128)(2,1)S(1)}, u32[]{:S(2)}) copy-start(bf16[1024,1024]{1,0:T(8,128)(2,1)S(1)} %get-tuple-element.75.second_ref) | copy-start | bytes 6291460
  98.6 1.6 %copy-start.9 = (bf16[1024,1024]{1,0:T(8,128)(2,1)S(1)}, bf16[1024,1024]{1,0:T(8,128)(2,1)}, u32[]{:S(2)}) copy-start(bf16[1024,1024]{1,0:T(8,128)(2,1)} %copy-done.8) | copy-start | bytes 6291460
  106.2 13.7 %all-to-all-start.1 = ((bf16[8,128,128]{2,1,0:T(8,128)(2,1)}), bf16[8,128,128]{2,1,0:T(8,128)(2,1)S(1)}, u32[]{:S(2)}, u32[]{:S(2)}) async-start(bf16[8,128,128]{2,1,0:T(8,128)(2,1)} %get-tuple-element.73), calls=%async_computation.1 | async-start | bytes 524288 | tf_op jit(solution)/shard_map/all_to_all | solution.py:473
  110.2 1.6 %copy-start.5 = (bf16[1024,1024]{1,0:T(8,128)(2,1)S(1)}, bf16[1024,1024]{1,0:T(8,128)(2,1)}, u32[]{:S(2)}) copy-start(bf16[1024,1024]{1,0:T(8,128)(2,1)} %copy-done.4) | copy-start | bytes 6291460
  111.8 1.6 %copy-start.7 = (bf16[1024,1024]{1,0:T(8,128)(2,1)S(1)}, bf16[1024,1024]{1,0:T(8,128)(2,1)}, u32[]{:S(2)}) copy-start(bf16[1024,1024]{1,0:T(8,128)(2,1)} %copy-done.6) | copy-start | bytes 6291460
  120.4 1.3 collective-permute-start.16
  121.7 5.4 %collective-permute-start.17 = (f32[16,128]{1,0:T(8,128)S(1)}, f32[16,128]{1,0:T(8,128)S(1)}, u32[]{:S(2)}, u32[]{:S(2)}) collective-permute-start(f32[16,128]{1,0:T(8,128)S(1)} %add.25), channel_id=1, source_target_pairs={{0,2},{2,4},{4,6},{6,0},{1,3},{3,5},{5,7},{7,1},{8,10},{10,12},{12... | collective-permute-start | bytes 24584 | tf_op jit(solution)/shard_map/ppermute | solution.py:20
  121.9 5.3 %collective-permute-start.18 = (f32[16,128]{1,0:T(8,128)S(1)}, f32[16,128]{1,0:T(8,128)S(1)}, u32[]{:S(2)}, u32[]{:S(2)}) collective-permute-start(f32[16,128]{1,0:T(8,128)S(1)} %add.25), channel_id=1, source_target_pairs={{0,4},{2,6},{4,0},{6,2},{1,5},{3,7},{5,1},{7,3},{8,12},{10,14},{12... | collective-permute-start | bytes 24584 | tf_op jit(solution)/shard_map/ppermute | solution.py:20
  124.1 3.7 %collective-permute-start.19 = (f32[16,128]{1,0:T(8,128)S(1)}, f32[16,128]{1,0:T(8,128)S(1)}, u32[]{:S(2)}, u32[]{:S(2)}) collective-permute-start(f32[16,128]{1,0:T(8,128)S(1)} %add.25), channel_id=1, source_target_pairs={{0,6},{2,0},{4,2},{6,4},{1,7},{3,1},{5,3},{7,5},{8,14},{10,8},{12,... | collective-permute-start | bytes 24584 | tf_op jit(solution)/shard_map/ppermute | solution.py:20
  (1 other events, 1.0 us)
Sparse Core Ops, SparseCore 0:
  14.4 43.6 all-gather.1
